TPU v7x, 32 devices: a whole 2x2x4 slice. The times are simulated.
32 devices in a mesh: ctx: 16 (over z, y, x), fsdp: 2 (over core).
Axes of the slice: x: 2, y: 2, z: 4, core: 2. Of those that a mesh axis runs over, the one named last changes fastest.
Arguments:
- x_in: bfloat16 [4, 1024, 576], P('fsdp', 'ctx')
- w_query: bfloat16 [576, 576], P('fsdp'), may hold values from -0.25 to 0.25
- w_key: bfloat16 [576, 192], P('fsdp'), may hold values from -0.25 to 0.25
- w_value: bfloat16 [576, 192], P('fsdp'), may hold values from -0.25 to 0.25
- w_out: bfloat16 [576, 576], P('fsdp'), may hold values from -6 to 6
- attn_gain: bfloat16 [576], P('fsdp'), may hold values from 0.5 to 1.5
- w_gate: bfloat16 [576, 1536], P('fsdp'), may hold values from -0.25 to 0.25
- w_up: bfloat16 [576, 1536], P('fsdp'), may hold values from -0.25 to 0.25
- w_down: bfloat16 [1536, 576], P('fsdp'), may hold values from -0.15625 to 0.15625
- mlp_gain: bfloat16 [576], P('fsdp'), may hold values from 0.5 to 1.5
- block_of_slot: int32 [32], replicated, may hold values from 0 to 31, as said below
- out_grad: bfloat16 [4, 1024, 576], P('fsdp', 'ctx'), may hold values from -6 to 6
Outputs:
- y_out: bfloat16 [4, 1024, 576], P('fsdp', 'ctx')
- x_grad: bfloat16 [4, 1024, 576], P('fsdp', 'ctx')
- grad_w_query: float32 [576, 576], P('fsdp')
- grad_w_key: float32 [576, 192], P('fsdp')
- grad_w_value: float32 [576, 192], P('fsdp')
- grad_w_out: float32 [576, 576], P('fsdp')
- grad_attn_gain: float32 [576], P('fsdp')
- grad_w_gate: float32 [576, 1536], P('fsdp')
- grad_w_up: float32 [576, 1536], P('fsdp')
- grad_w_down: float32 [1536, 576], P('fsdp')
- grad_mlp_gain: float32 [576], P('fsdp')
Inputs may be any that keep to these rules, and one draw needn't show every extreme that they name: `block_of_slot`: the entries are a permutation of 0 to 31 and entries 2 i and 2 i + 1 sum to 31, so slots 2 i and 2 i + 1 hold a block from the front of the sequence and its mirror from the back.
All inputs are finite; a program needn't handle non-finite values.
Results may differ from a plain program's by a relative error of at most 0.025.
Values may be sent and summed in bfloat16 or wider, within the bound.
A program may use at most 128 MiB of HBM per device.

v0:
```python
import jax
import jax.numpy as jnp
from jax import lax
from jax.sharding import PartitionSpec as P

HEADS = 9
KV_HEADS = 3
HEAD_DIM = 64


epsilon = 1e-05
theta_base = 100000.0
masked_value = -1e30


def shifted(block, axis, distance):
    devices = range(lax.axis_size(axis))
    route = [((i - distance) % len(devices), i) for i in devices]
    return lax.ppermute(block, axis, route)


def make_tables(positions):
    half_dim = HEAD_DIM // 2
    frequency = theta_base ** (-2.0 * jnp.arange(half_dim, dtype=jnp.float32) / HEAD_DIM)
    angles = positions.astype(jnp.float32)[:, None] * frequency[None, :]
    return (jnp.cos(angles), jnp.sin(angles))


def rotate(values, cosine, sine):
    half_dim = values.shape[-1] // 2
    first_half = values[..., :half_dim]
    second_half = values[..., half_dim:]
    cos_rows = cosine[:, None, :]
    sin_rows = sine[:, None, :]
    return jnp.concatenate(
        [
            first_half * cos_rows - second_half * sin_rows,
            second_half * cos_rows + first_half * sin_rows,
        ],
        axis=-1,
    )


def rotate_back(grads, cosine, sine):
    half_dim = grads.shape[-1] // 2
    first_half = grads[..., :half_dim]
    second_half = grads[..., half_dim:]
    cos_rows = cosine[:, None, :]
    sin_rows = sine[:, None, :]
    return jnp.concatenate(
        [
            first_half * cos_rows + second_half * sin_rows,
            second_half * cos_rows - first_half * sin_rows,
        ],
        axis=-1,
    )


def slot_positions(block_of_slot, offset, count_rows, half_len):
    row_ids = offset + jnp.arange(count_rows, dtype=jnp.int32)
    slot_ids = row_ids // half_len
    slot_match = slot_ids[:, None] == jnp.arange(block_of_slot.shape[0], dtype=jnp.int32)[None, :]
    owners = jnp.sum(jnp.where(slot_match, block_of_slot[None, :], 0), axis=1)
    return owners * half_len + row_ids % half_len


def norm_forward(values, gain_vec):
    inverse = lax.rsqrt(jnp.mean(values * values, axis=-1, keepdims=True) + epsilon)
    scaled = values * inverse
    return (scaled * gain_vec, scaled, inverse)


def norm_backward(grad_output, gain_vec, scaled, inverse):
    grad_scaled = grad_output * gain_vec
    grad_input = inverse * (
        grad_scaled - scaled * jnp.mean(grad_scaled * scaled, axis=-1, keepdims=True)
    )
    grad_gain = jnp.sum(grad_output * scaled, axis=0)
    return (grad_input, grad_gain)


def local(
    x_in,
    w_query,
    w_key,
    w_value,
    w_out,
    attn_gain,
    w_gate,
    w_up,
    w_down,
    mlp_gain,
    block_of_slot,
    out_grad,
):
    gathered = (
        lax.all_gather(w_query, "fsdp", axis=0, tiled=True),
        lax.all_gather(w_key, "fsdp", axis=0, tiled=True),
        lax.all_gather(w_value, "fsdp", axis=0, tiled=True),
        lax.all_gather(w_out, "fsdp", axis=0, tiled=True),
        lax.all_gather(attn_gain, "fsdp", axis=0, tiled=True),
        lax.all_gather(w_gate, "fsdp", axis=0, tiled=True),
        lax.all_gather(w_up, "fsdp", axis=0, tiled=True),
        lax.all_gather(w_down, "fsdp", axis=0, tiled=True),
        lax.all_gather(mlp_gain, "fsdp", axis=0, tiled=True),
    )
    (
        full_query,
        full_key,
        full_value,
        full_out,
        gain_attn,
        full_gate,
        full_up,
        full_down,
        gain_mlp,
    ) = gathered
    gain_attn_f = gain_attn.astype(jnp.float32)
    gain_mlp_f = gain_mlp.astype(jnp.float32)
    seq_count, tok_count, model_width = x_in.shape
    group_size = HEADS // KV_HEADS
    half_len = tok_count // 2
    rows_all = seq_count * tok_count
    ctx_count = lax.axis_size("ctx")
    score_scale = HEAD_DIM ** (-0.5)
    my_offset = lax.axis_index("ctx") * tok_count
    query_pos = slot_positions(block_of_slot, my_offset, tok_count, half_len)
    cosine, sine = make_tables(query_pos)
    inputs = x_in.astype(jnp.float32).reshape(rows_all, model_width)
    normed_f, scaled_one, inverse_one = norm_forward(inputs, gain_attn_f)
    normed = normed_f.astype(jnp.bfloat16)
    query_f = jnp.dot(normed, full_query, preferred_element_type=jnp.float32).reshape(
        seq_count, tok_count, HEADS, HEAD_DIM
    )
    queries = (
        rotate(query_f, cosine, sine)
        .astype(jnp.bfloat16)
        .reshape(seq_count, tok_count, KV_HEADS, group_size, HEAD_DIM)
    )
    key_f = jnp.dot(normed, full_key, preferred_element_type=jnp.float32).reshape(
        seq_count, tok_count, KV_HEADS, HEAD_DIM
    )
    key_rows = rotate(key_f, cosine, sine).astype(jnp.bfloat16)
    value_rows = (
        jnp.dot(normed, full_value, preferred_element_type=jnp.float32)
        .astype(jnp.bfloat16)
        .reshape(seq_count, tok_count, KV_HEADS, HEAD_DIM)
    )
    stat_shape = (seq_count, KV_HEADS, group_size, tok_count)
    running_max = jnp.full(stat_shape, masked_value, jnp.float32)
    key_part = lax.all_gather(key_rows, "ctx", axis=1, tiled=True)
    value_part = lax.all_gather(value_rows, "ctx", axis=1, tiled=True)
    key_pos = slot_positions(block_of_slot, jnp.int32(0), key_part.shape[1], half_len)
    visible = query_pos[:, None] >= key_pos[None, :]
    scores = (
        jnp.einsum("sqkgd,snkd->skgqn", queries, key_part, preferred_element_type=jnp.float32)
        * score_scale
    )
    scores = jnp.where(visible, scores, masked_value)
    new_max = jnp.maximum(running_max, jnp.max(scores, axis=-1))
    weights = jnp.where(visible, jnp.exp(scores - new_max[..., None]), 0.0)
    totals = jnp.sum(weights, axis=-1)
    weighted_sum = jnp.einsum(
        "skgqn,snkd->skgqd",
        weights.astype(jnp.bfloat16),
        value_part,
        preferred_element_type=jnp.float32,
    )
    running_max, totals, weighted_sum = (new_max, totals, weighted_sum)
    log_total = running_max + jnp.log(totals)
    attended_f = weighted_sum / totals[..., None]
    attended = (
        attended_f.transpose(0, 3, 1, 2, 4).reshape(rows_all, model_width).astype(jnp.bfloat16)
    )
    hidden_state = inputs + jnp.dot(attended, full_out, preferred_element_type=jnp.float32)
    normed_two_f, scaled_two, inverse_two = norm_forward(hidden_state, gain_mlp_f)
    normed_two = normed_two_f.astype(jnp.bfloat16)
    gate_vals = jnp.dot(normed_two, full_gate, preferred_element_type=jnp.float32)
    up_vals = jnp.dot(normed_two, full_up, preferred_element_type=jnp.float32)
    sigmoid_gate = jax.nn.sigmoid(gate_vals)
    activated = gate_vals * sigmoid_gate
    inner_rows = (activated * up_vals).astype(jnp.bfloat16)
    result = hidden_state + jnp.dot(inner_rows, full_down, preferred_element_type=jnp.float32)
    y_out = result.reshape(seq_count, tok_count, model_width).astype(jnp.bfloat16)
    grad_top = out_grad.reshape(rows_all, model_width)
    grad_residual = grad_top.astype(jnp.float32)
    grad_wdown = jnp.einsum("rf,rd->fd", inner_rows, grad_top, preferred_element_type=jnp.float32)
    grad_inner = jnp.einsum("rd,fd->rf", grad_top, full_down, preferred_element_type=jnp.float32)
    grad_gate = (
        grad_inner * up_vals * sigmoid_gate * (1.0 + gate_vals * (1.0 - sigmoid_gate))
    ).astype(jnp.bfloat16)
    grad_up = (grad_inner * activated).astype(jnp.bfloat16)
    grad_wgate = jnp.einsum("rd,rf->df", normed_two, grad_gate, preferred_element_type=jnp.float32)
    grad_wup = jnp.einsum("rd,rf->df", normed_two, grad_up, preferred_element_type=jnp.float32)
    grad_normed_two = jnp.einsum(
        "rf,df->rd", grad_gate, full_gate, preferred_element_type=jnp.float32
    ) + jnp.einsum("rf,df->rd", grad_up, full_up, preferred_element_type=jnp.float32)
    grad_hidden_norm, grad_gain_mlp = norm_backward(
        grad_normed_two, gain_mlp_f, scaled_two, inverse_two
    )
    grad_hidden = grad_residual + grad_hidden_norm
    grad_branch = grad_hidden.astype(jnp.bfloat16)
    grad_wout = jnp.einsum("ri,rj->ij", attended, grad_branch, preferred_element_type=jnp.float32)
    grad_attended = jnp.einsum(
        "rj,ij->ri", grad_branch, full_out, preferred_element_type=jnp.float32
    ).astype(jnp.bfloat16)
    grad_heads = grad_attended.reshape(
        seq_count, tok_count, KV_HEADS, group_size, HEAD_DIM
    ).transpose(0, 2, 3, 1, 4)
    row_delta = jnp.sum(grad_heads.astype(jnp.float32) * attended_f, axis=-1)

    def block_grads(key_part, value_part, offset):
        key_pos = slot_positions(block_of_slot, offset, key_part.shape[1], half_len)
        visible = query_pos[:, None] >= key_pos[None, :]
        scores = (
            jnp.einsum("sqkgd,snkd->skgqn", queries, key_part, preferred_element_type=jnp.float32)
            * score_scale
        )
        weights = jnp.where(visible, jnp.exp(scores - log_total[..., None]), 0.0)
        grad_value_part = jnp.einsum(
            "skgqn,skgqd->snkd",
            weights.astype(jnp.bfloat16),
            grad_heads,
            preferred_element_type=jnp.float32,
        )
        grad_weights = jnp.einsum(
            "skgqd,snkd->skgqn", grad_heads, value_part, preferred_element_type=jnp.float32
        )
        grad_scores = (weights * (grad_weights - row_delta[..., None])).astype(jnp.bfloat16)
        grad_query_part = jnp.einsum(
            "skgqn,snkd->skgqd", grad_scores, key_part, preferred_element_type=jnp.float32
        )
        grad_key_part = (
            jnp.einsum(
                "skgqn,sqkgd->snkd", grad_scores, queries, preferred_element_type=jnp.float32
            )
            * score_scale
        )
        return (grad_query_part, grad_key_part, grad_value_part)

    grad_query_init = jnp.zeros(stat_shape + (HEAD_DIM,), jnp.float32)
    kv_zero = jnp.zeros(key_rows.shape, jnp.float32)

    def one_hop(hop_index, loop_state):
        key_part, value_part, grad_query, grad_key, grad_value = loop_state
        source = (lax.axis_index("ctx") - hop_index) % ctx_count
        grad_query_part, grad_key_part, grad_value_part = block_grads(
            key_part, value_part, source * tok_count
        )
        key_part, value_part = shifted((key_part, value_part), "ctx", 1)
        grad_key, grad_value = (
            shifted((grad_key + grad_key_part).astype(jnp.bfloat16), "ctx", 1).astype(jnp.float32),
            shifted((grad_value + grad_value_part).astype(jnp.bfloat16), "ctx", 1).astype(
                jnp.float32
            ),
        )
        return (key_part, value_part, grad_query + grad_query_part, grad_key, grad_value)

    loop_state = lax.fori_loop(
        0, ctx_count - 1, one_hop, (key_rows, value_rows, grad_query_init, kv_zero, kv_zero)
    )
    key_part, value_part, grad_query, grad_key, grad_value = loop_state
    source = (lax.axis_index("ctx") + 1) % ctx_count
    grad_query_part, grad_key_part, grad_value_part = block_grads(
        key_part, value_part, source * tok_count
    )
    grad_query = grad_query + grad_query_part
    grad_key, grad_value = (
        shifted((grad_key + grad_key_part).astype(jnp.bfloat16), "ctx", 1).astype(jnp.float32),
        shifted((grad_value + grad_value_part).astype(jnp.bfloat16), "ctx", 1).astype(jnp.float32),
    )
    grad_query_rows = (
        (grad_query * score_scale)
        .transpose(0, 3, 1, 2, 4)
        .reshape(seq_count, tok_count, HEADS, HEAD_DIM)
    )
    grad_query_low = (
        rotate_back(grad_query_rows, cosine, sine)
        .astype(jnp.bfloat16)
        .reshape(rows_all, model_width)
    )
    grad_key_low = (
        rotate_back(grad_key, cosine, sine)
        .astype(jnp.bfloat16)
        .reshape(rows_all, KV_HEADS * HEAD_DIM)
    )
    grad_value_low = grad_value.astype(jnp.bfloat16).reshape(rows_all, KV_HEADS * HEAD_DIM)
    grad_wquery = jnp.einsum(
        "rd,re->de", normed, grad_query_low, preferred_element_type=jnp.float32
    )
    grad_wkey = jnp.einsum("rd,re->de", normed, grad_key_low, preferred_element_type=jnp.float32)
    grad_wvalue = jnp.einsum(
        "rd,re->de", normed, grad_value_low, preferred_element_type=jnp.float32
    )
    grad_normed = jnp.einsum(
        "re,de->rd", grad_query_low, full_query, preferred_element_type=jnp.float32
    )
    grad_normed = grad_normed + jnp.einsum(
        "re,de->rd", grad_key_low, full_key, preferred_element_type=jnp.float32
    )
    grad_normed = grad_normed + jnp.einsum(
        "re,de->rd", grad_value_low, full_value, preferred_element_type=jnp.float32
    )
    grad_input_norm, grad_gain_attn = norm_backward(
        grad_normed, gain_attn_f, scaled_one, inverse_one
    )
    x_grad = (
        (grad_hidden + grad_input_norm)
        .astype(jnp.bfloat16)
        .reshape(seq_count, tok_count, model_width)
    )
    owned_grads = (
        lax.psum_scatter(
            grad_wquery.astype(jnp.bfloat16), "fsdp", scatter_dimension=0, tiled=True
        ).astype(jnp.float32),
        lax.psum_scatter(
            grad_wkey.astype(jnp.bfloat16), "fsdp", scatter_dimension=0, tiled=True
        ).astype(jnp.float32),
        lax.psum_scatter(
            grad_wvalue.astype(jnp.bfloat16), "fsdp", scatter_dimension=0, tiled=True
        ).astype(jnp.float32),
        lax.psum_scatter(
            grad_wout.astype(jnp.bfloat16), "fsdp", scatter_dimension=0, tiled=True
        ).astype(jnp.float32),
        lax.psum_scatter(
            grad_gain_attn.astype(jnp.bfloat16), "fsdp", scatter_dimension=0, tiled=True
        ).astype(jnp.float32),
        lax.psum_scatter(
            grad_wgate.astype(jnp.bfloat16), "fsdp", scatter_dimension=0, tiled=True
        ).astype(jnp.float32),
        lax.psum_scatter(
            grad_wup.astype(jnp.bfloat16), "fsdp", scatter_dimension=0, tiled=True
        ).astype(jnp.float32),
        lax.psum_scatter(
            grad_wdown.astype(jnp.bfloat16), "fsdp", scatter_dimension=0, tiled=True
        ).astype(jnp.float32),
        lax.psum_scatter(
            grad_gain_mlp.astype(jnp.bfloat16), "fsdp", scatter_dimension=0, tiled=True
        ).astype(jnp.float32),
    )
    summed_grads = (
        lax.psum(owned_grads[0].astype(jnp.bfloat16), "ctx").astype(jnp.float32),
        lax.psum(owned_grads[1].astype(jnp.bfloat16), "ctx").astype(jnp.float32),
        lax.psum(owned_grads[2].astype(jnp.bfloat16), "ctx").astype(jnp.float32),
        lax.psum(owned_grads[3].astype(jnp.bfloat16), "ctx").astype(jnp.float32),
        lax.psum(owned_grads[4].astype(jnp.bfloat16), "ctx").astype(jnp.float32),
        lax.psum(owned_grads[5].astype(jnp.bfloat16), "ctx").astype(jnp.float32),
        lax.psum(owned_grads[6].astype(jnp.bfloat16), "ctx").astype(jnp.float32),
        lax.psum(owned_grads[7].astype(jnp.bfloat16), "ctx").astype(jnp.float32),
        lax.psum(owned_grads[8].astype(jnp.bfloat16), "ctx").astype(jnp.float32),
    )
    return (
        y_out,
        x_grad,
        summed_grads[0],
        summed_grads[1],
        summed_grads[2],
        summed_grads[3],
        summed_grads[4],
        summed_grads[5],
        summed_grads[6],
        summed_grads[7],
        summed_grads[8],
    )


def solution(mesh):
    placed = (
        P("fsdp", "ctx", None),
        P("fsdp", None),
        P("fsdp", None),
        P("fsdp", None),
        P("fsdp", None),
        P("fsdp"),
        P("fsdp", None),
        P("fsdp", None),
        P("fsdp", None),
        P("fsdp"),
        P(),
        P("fsdp", "ctx", None),
    )
    return jax.shard_map(
        local,
        mesh=mesh,
        in_specs=placed,
        out_specs=(
            P("fsdp", "ctx", None),
            P("fsdp", "ctx", None),
            P("fsdp", None),
            P("fsdp", None),
            P("fsdp", None),
            P("fsdp", None),
            P("fsdp"),
            P("fsdp", None),
            P("fsdp", None),
            P("fsdp", None),
            P("fsdp"),
        ),
        check_vma=False,
    )
```

profile of v0, /device:TPU:27, one launch (start us, length us, event | category | flops | bytes accessed | tf_op | source)
XLA Modules:
  0.0 651.4 jit_solution(17104645423890764450)
XLA Ops:
  18.6 42.7 %all_gather.35 = bf16[2,1024,3,64]{3,0,2,1:T(2,128)(2,1)} all-gather(bf16[2,64,3,64]{3,0,2,1:T(2,128)(2,1)S(1)} %copy.115), channel_id=1, replica_groups=mesh['ctx'=16,'fsdp'=2] {'ctx'}, dimensions={1}, use_global_device_ids=true | all-gather | bytes 835584 | tf_op jit(solution)/shard_map/all_gather | solution.py:151
  61.3 7.7 %all_gather.36 = bf16[576,576]{1,0:T(8,128)(2,1)S(1)} all-gather(bf16[288,576]{1,0:T(8,128)(2,1)S(1)} %copy-done.35), channel_id=1, replica_groups=mesh['ctx'=16,'fsdp'=2] {'fsdp'}, dimensions={0}, use_global_device_ids=true | all-gather | bytes 995328 | tf_op jit(solution)/shard_map/all_gather | solution.py:97
  72.1 3.1 fusion.17
  77.9 47.0 %all_gather.38 = bf16[2,1024,3,64]{3,0,2,1:T(2,128)(2,1)S(1)} all-gather(bf16[2,64,3,64]{3,0,2,1:T(2,128)(2,1)S(1)} %copy.121), channel_id=1, replica_groups=mesh['ctx'=16,'fsdp'=2] {'ctx'}, dimensions={1}, use_global_device_ids=true | all-gather | bytes 835584 | tf_op jit(solution)/shard_map/all_gather | solution.py:152
  124.9 3.9 fusion.18
  131.9 9.8 %all_gather.39 = bf16[576,576]{1,0:T(8,128)(2,1)S(1)} all-gather(bf16[288,576]{1,0:T(8,128)(2,1)S(1)} %copy-done.36), channel_id=1, replica_groups=mesh['ctx'=16,'fsdp'=2] {'fsdp'}, dimensions={0}, use_global_device_ids=true | all-gather | bytes 995328 | tf_op jit(solution)/shard_map/all_gather | solution.py:100
  152.6 3.5 multiply_convert_fusion
  161.3 198.5 %while.25 = (s32[]{:T(128)}, bf16[2,64,3,64]{3,1,2,0:T(8,128)(2,1)S(1)}, bf16[2,64,3,64]{3,1,2,0:T(8,128)(2,1)S(1)}, f32[2,3,3,64,64]{4,3,2,1,0:T(8,128)S(1)}, f...) while((s32[]{:T(128)}, ...), condition=%wide.region_10.11_spmd.clone, body=%wide.region_8.10_spmd.clone.sunk | while | flops 48082768 | bytes 4246918 | solution.py:259
  177.6 4.4 collective-permute-start.2
  190.9 5.2 collective-permute-start.2
  205.0 5.1 collective-permute-start.2
  219.0 3.6 collective-permute-start.2
  224.2 3.1 collective-permute-done.3
  231.6 4.9 collective-permute-start.2
  245.5 4.9 collective-permute-start.2
  259.3 4.5 collective-permute-start.2
  277.1 3.1 collective-permute-done.3
  296.0 3.6 collective-permute-start.2
  304.2 3.0 collective-permute-start
  310.5 3.5 collective-permute-start.2
  323.8 4.3 collective-permute-start.2
  336.9 5.1 collective-permute-start.2
  350.9 5.0 collective-permute-start.2
  379.6 13.7 %reduce-scatter.12.cloned.1.call-done = bf16[288,192]{1,0:T(8,128)(2,1)} async-done(((bf16[576,192]{1,0:T(8,128)(2,1)}), bf16[288,192]{1,0:T(8,128)(2,1)}) %reduce-scatter.12.cloned.1.call-update) | async-done | bytes 110608 | tf_op jit(solution)/shard_map/reduce_scatter | solution.py:319
  393.4 11.0 %reduce-scatter.10.cloned.1.call-done = bf16[288,192]{1,0:T(8,128)(2,1)} async-done(((bf16[576,192]{1,0:T(8,128)(2,1)}), bf16[288,192]{1,0:T(8,128)(2,1)}) %reduce-scatter.10.cloned.1.call-update) | async-done | bytes 110608 | tf_op jit(solution)/shard_map/reduce_scatter | solution.py:316
  404.3 11.5 %reduce-scatter.14.cloned.1.call-done = bf16[288,576]{1,0:T(8,128)(2,1)} async-done(((bf16[576,576]{1,0:T(8,128)(2,1)}), bf16[288,576]{1,0:T(8,128)(2,1)}) %reduce-scatter.14.cloned.1.call-update) | async-done | bytes 331792 | tf_op jit(solution)/shard_map/reduce_scatter | solution.py:322
  415.8 12.2 %reduce-scatter.8.cloned.1.call-done = bf16[288,576]{1,0:T(8,128)(2,1)} async-done(((bf16[576,576]{1,0:T(8,128)(2,1)}), bf16[288,576]{1,0:T(8,128)(2,1)}) %reduce-scatter.8.cloned.1.call-update) | async-done | bytes 331792 | tf_op jit(solution)/shard_map/reduce_scatter | solution.py:313
  428.0 13.3 %reduce-scatter.18.cloned.1.call-done = bf16[288,1536]{1,0:T(8,128)(2,1)} async-done(((bf16[576,1536]{1,0:T(8,128)(2,1)}), bf16[288,1536]{1,0:T(8,128)(2,1)}) %reduce-scatter.18.cloned.1.call-update) | async-done | bytes 884752 | tf_op jit(solution)/shard_map/reduce_scatter | solution.py:331
  441.3 13.4 %reduce-scatter.16.cloned.1.call-done = bf16[288,1536]{1,0:T(8,128)(2,1)} async-done(((bf16[576,1536]{1,0:T(8,128)(2,1)}), bf16[288,1536]{1,0:T(8,128)(2,1)}) %reduce-scatter.16.cloned.1.call-update) | async-done | bytes 884752 | tf_op jit(solution)/shard_map/reduce_scatter | solution.py:328
  454.8 13.2 %reduce-scatter.20.cloned.1.call-done = bf16[768,576]{0,1:T(8,128)(2,1)} async-done(((bf16[1536,576]{0,1:T(8,128)(2,1)}), bf16[768,576]{0,1:T(8,128)(2,1)}) %reduce-scatter.20.cloned.1.call-update) | async-done | bytes 884752 | tf_op jit(solution)/shard_map/reduce_scatter | solution.py:334
  475.3 28.6 %all-reduce.4 = (bf16[288]{0:T(512)(128)(2,1)S(1)}, bf16[288]{0:T(512)(128)(2,1)S(1)}) all-reduce(bf16[288]{0:T(512)(128)(2,1)S(1)} %dynamic-slice.3, bf16[288]{0:T(512)(128)(2,1)S(1)} %dynamic-slice.5), channel_id=1, replica_groups=mesh['ctx'=16,'fsdp'=2] {'ctx'}, use_global_device_ids=true, to_apply=%region_23.24 | all-reduce | flops 576 | bytes 2304 | tf_op jit(solution)/shard_map/psum | solution.py:346
  506.1 130.0 %all-reduce.10.cloned.1.call-done = (bf16[288,576]{1,0:T(8,128)(2,1)}, bf16[288,192]{1,0:T(8,128)(2,1)}, bf16[288,192]{1,0:T(8,128)(2,1)}, bf16[288,576]{1,0:T(8...) async-done(((bf16[288,576]{1,0:T(8,128)(2,1)}, bf16[288,192]{1,0:T(8,128)(2,1)}, bf16[288,192]{1,0:T(8,128)(2,1)}, ...) | async-done | bytes 3538960 | tf_op jit(solution)/shard_map/psum | solution.py:342
  (541 shorter events, 205.7 us)
Async XLA Ops:
  7.2 139.6 %all-gather.4.cloned.1.call-start = ((), (), s32[]{:S(2)}) async-start(), calls=%async_computation.7 | async-start | bytes 2654208 | tf_op jit(solution)/shard_map/all_gather | solution.py:102
  8.0 141.8 %all-gather.6.cloned.1.call-start = ((), (), s32[]{:S(2)}) async-start(), calls=%async_computation.8 | async-start | bytes 2654208 | tf_op jit(solution)/shard_map/all_gather | solution.py:103
  8.7 143.9 %all-gather.8.cloned.1.call-start = ((), (), s32[]{:S(2)}) async-start(), calls=%async_computation.9 | async-start | bytes 2654208 | tf_op jit(solution)/shard_map/all_gather | solution.py:104
  9.4 383.9 %reduce-scatter.12.cloned.1.call-start = ((), (), s32[]{:S(2)}) async-start(), calls=%async_computation.12 | async-start | bytes 442368 | tf_op jit(solution)/shard_map/reduce_scatter | solution.py:319
  172.0 13.8 %collective-permute-start = (bf16[2,64,3,64]{3,1,2,0:T(8,128)(2,1)S(1)}, bf16[2,64,3,64]{3,1,2,0:T(8,128)(2,1)S(1)}, u32[]{:S(2)}, u32[]{:S(2)}) collective-permute-start(bf16[2,64,3,64]{3,1,2,0:T(8,128)(2,1)S(1)} %copy.200), channel_id=1, source_target_pairs={{30,0},{0,2},{2,4},{4,6},{6,8},{8,10},{10,12},{12,14},{14,16},{16,... | collective-permute-start | bytes 147464 | tf_op jit(solution)/shard_map/while/body/eval_jaxpr/ppermute | solution.py:19
  185.9 14.1 %collective-permute-start = (bf16[2,64,3,64]{3,1,2,0:T(8,128)(2,1)S(1)}, bf16[2,64,3,64]{3,1,2,0:T(8,128)(2,1)S(1)}, u32[]{:S(2)}, u32[]{:S(2)}) collective-permute-start(bf16[2,64,3,64]{3,1,2,0:T(8,128)(2,1)S(1)} %copy.200), channel_id=1, source_target_pairs={{30,0},{0,2},{2,4},{4,6},{6,8},{8,10},{10,12},{12,14},{14,16},{16,... | collective-permute-start | bytes 147464 | tf_op jit(solution)/shard_map/while/body/eval_jaxpr/ppermute | solution.py:19
  187.5 12.4 %collective-permute-start.1 = (bf16[2,64,3,64]{3,1,2,0:T(8,128)(2,1)S(1)}, bf16[2,64,3,64]{3,1,2,0:T(8,128)(2,1)S(1)}, u32[]{:S(2)}, u32[]{:S(2)}) collective-permute-start(bf16[2,64,3,64]{3,1,2,0:T(8,128)(2,1)S(1)} %copy.201), channel_id=1, source_target_pairs={{30,0},{0,2},{2,4},{4,6},{6,8},{8,10},{10,12},{12,14},{14,16},{16,... | collective-permute-start | bytes 147464 | tf_op jit(solution)/shard_map/while/body/eval_jaxpr/ppermute | solution.py:19
  200.0 13.9 %collective-permute-start = (bf16[2,64,3,64]{3,1,2,0:T(8,128)(2,1)S(1)}, bf16[2,64,3,64]{3,1,2,0:T(8,128)(2,1)S(1)}, u32[]{:S(2)}, u32[]{:S(2)}) collective-permute-start(bf16[2,64,3,64]{3,1,2,0:T(8,128)(2,1)S(1)} %copy.200), channel_id=1, source_target_pairs={{30,0},{0,2},{2,4},{4,6},{6,8},{8,10},{10,12},{12,14},{14,16},{16,... | collective-permute-start | bytes 147464 | tf_op jit(solution)/shard_map/while/body/eval_jaxpr/ppermute | solution.py:19
  201.7 12.3 %collective-permute-start.1 = (bf16[2,64,3,64]{3,1,2,0:T(8,128)(2,1)S(1)}, bf16[2,64,3,64]{3,1,2,0:T(8,128)(2,1)S(1)}, u32[]{:S(2)}, u32[]{:S(2)}) collective-permute-start(bf16[2,64,3,64]{3,1,2,0:T(8,128)(2,1)S(1)} %copy.201), channel_id=1, source_target_pairs={{30,0},{0,2},{2,4},{4,6},{6,8},{8,10},{10,12},{12,14},{14,16},{16,... | collective-permute-start | bytes 147464 | tf_op jit(solution)/shard_map/while/body/eval_jaxpr/ppermute | solution.py:19
  214.0 13.4 %collective-permute-start = (bf16[2,64,3,64]{3,1,2,0:T(8,128)(2,1)S(1)}, bf16[2,64,3,64]{3,1,2,0:T(8,128)(2,1)S(1)}, u32[]{:S(2)}, u32[]{:S(2)}) collective-permute-start(bf16[2,64,3,64]{3,1,2,0:T(8,128)(2,1)S(1)} %copy.200), channel_id=1, source_target_pairs={{30,0},{0,2},{2,4},{4,6},{6,8},{8,10},{10,12},{12,14},{14,16},{16,... | collective-permute-start | bytes 147464 | tf_op jit(solution)/shard_map/while/body/eval_jaxpr/ppermute | solution.py:19
  215.6 11.7 %collective-permute-start.1 = (bf16[2,64,3,64]{3,1,2,0:T(8,128)(2,1)S(1)}, bf16[2,64,3,64]{3,1,2,0:T(8,128)(2,1)S(1)}, u32[]{:S(2)}, u32[]{:S(2)}) collective-permute-start(bf16[2,64,3,64]{3,1,2,0:T(8,128)(2,1)S(1)} %copy.201), channel_id=1, source_target_pairs={{30,0},{0,2},{2,4},{4,6},{6,8},{8,10},{10,12},{12,14},{14,16},{16,... | collective-permute-start | bytes 147464 | tf_op jit(solution)/shard_map/while/body/eval_jaxpr/ppermute | solution.py:19
  227.4 13.4 %collective-permute-start = (bf16[2,64,3,64]{3,1,2,0:T(8,128)(2,1)S(1)}, bf16[2,64,3,64]{3,1,2,0:T(8,128)(2,1)S(1)}, u32[]{:S(2)}, u32[]{:S(2)}) collective-permute-start(bf16[2,64,3,64]{3,1,2,0:T(8,128)(2,1)S(1)} %copy.200), channel_id=1, source_target_pairs={{30,0},{0,2},{2,4},{4,6},{6,8},{8,10},{10,12},{12,14},{14,16},{16,... | collective-permute-start | bytes 147464 | tf_op jit(solution)/shard_map/while/body/eval_jaxpr/ppermute | solution.py:19
  228.1 12.7 %collective-permute-start.1 = (bf16[2,64,3,64]{3,1,2,0:T(8,128)(2,1)S(1)}, bf16[2,64,3,64]{3,1,2,0:T(8,128)(2,1)S(1)}, u32[]{:S(2)}, u32[]{:S(2)}) collective-permute-start(bf16[2,64,3,64]{3,1,2,0:T(8,128)(2,1)S(1)} %copy.201), channel_id=1, source_target_pairs={{30,0},{0,2},{2,4},{4,6},{6,8},{8,10},{10,12},{12,14},{14,16},{16,... | collective-permute-start | bytes 147464 | tf_op jit(solution)/shard_map/while/body/eval_jaxpr/ppermute | solution.py:19
  240.8 13.8 %collective-permute-start = (bf16[2,64,3,64]{3,1,2,0:T(8,128)(2,1)S(1)}, bf16[2,64,3,64]{3,1,2,0:T(8,128)(2,1)S(1)}, u32[]{:S(2)}, u32[]{:S(2)}) collective-permute-start(bf16[2,64,3,64]{3,1,2,0:T(8,128)(2,1)S(1)} %copy.200), channel_id=1, source_target_pairs={{30,0},{0,2},{2,4},{4,6},{6,8},{8,10},{10,12},{12,14},{14,16},{16,... | collective-permute-start | bytes 147464 | tf_op jit(solution)/shard_map/while/body/eval_jaxpr/ppermute | solution.py:19
  242.0 12.7 %collective-permute-start.1 = (bf16[2,64,3,64]{3,1,2,0:T(8,128)(2,1)S(1)}, bf16[2,64,3,64]{3,1,2,0:T(8,128)(2,1)S(1)}, u32[]{:S(2)}, u32[]{:S(2)}) collective-permute-start(bf16[2,64,3,64]{3,1,2,0:T(8,128)(2,1)S(1)} %copy.201), channel_id=1, source_target_pairs={{30,0},{0,2},{2,4},{4,6},{6,8},{8,10},{10,12},{12,14},{14,16},{16,... | collective-permute-start | bytes 147464 | tf_op jit(solution)/shard_map/while/body/eval_jaxpr/ppermute | solution.py:19
  254.7 12.9 %collective-permute-start = (bf16[2,64,3,64]{3,1,2,0:T(8,128)(2,1)S(1)}, bf16[2,64,3,64]{3,1,2,0:T(8,128)(2,1)S(1)}, u32[]{:S(2)}, u32[]{:S(2)}) collective-permute-start(bf16[2,64,3,64]{3,1,2,0:T(8,128)(2,1)S(1)} %copy.200), channel_id=1, source_target_pairs={{30,0},{0,2},{2,4},{4,6},{6,8},{8,10},{10,12},{12,14},{14,16},{16,... | collective-permute-start | bytes 147464 | tf_op jit(solution)/shard_map/while/body/eval_jaxpr/ppermute | solution.py:19
  255.9 11.8 %collective-permute-start.1 = (bf16[2,64,3,64]{3,1,2,0:T(8,128)(2,1)S(1)}, bf16[2,64,3,64]{3,1,2,0:T(8,128)(2,1)S(1)}, u32[]{:S(2)}, u32[]{:S(2)}) collective-permute-start(bf16[2,64,3,64]{3,1,2,0:T(8,128)(2,1)S(1)} %copy.201), channel_id=1, source_target_pairs={{30,0},{0,2},{2,4},{4,6},{6,8},{8,10},{10,12},{12,14},{14,16},{16,... | collective-permute-start | bytes 147464 | tf_op jit(solution)/shard_map/while/body/eval_jaxpr/ppermute | solution.py:19
  267.7 12.6 %collective-permute-start = (bf16[2,64,3,64]{3,1,2,0:T(8,128)(2,1)S(1)}, bf16[2,64,3,64]{3,1,2,0:T(8,128)(2,1)S(1)}, u32[]{:S(2)}, u32[]{:S(2)}) collective-permute-start(bf16[2,64,3,64]{3,1,2,0:T(8,128)(2,1)S(1)} %copy.200), channel_id=1, source_target_pairs={{30,0},{0,2},{2,4},{4,6},{6,8},{8,10},{10,12},{12,14},{14,16},{16,... | collective-permute-start | bytes 147464 | tf_op jit(solution)/shard_map/while/body/eval_jaxpr/ppermute | solution.py:19
  291.0 13.2 %collective-permute-start = (bf16[2,64,3,64]{3,1,2,0:T(8,128)(2,1)S(1)}, bf16[2,64,3,64]{3,1,2,0:T(8,128)(2,1)S(1)}, u32[]{:S(2)}, u32[]{:S(2)}) collective-permute-start(bf16[2,64,3,64]{3,1,2,0:T(8,128)(2,1)S(1)} %copy.200), channel_id=1, source_target_pairs={{30,0},{0,2},{2,4},{4,6},{6,8},{8,10},{10,12},{12,14},{14,16},{16,... | collective-permute-start | bytes 147464 | tf_op jit(solution)/shard_map/while/body/eval_jaxpr/ppermute | solution.py:19
  304.2 13.6 %collective-permute-start = (bf16[2,64,3,64]{3,1,2,0:T(8,128)(2,1)S(1)}, bf16[2,64,3,64]{3,1,2,0:T(8,128)(2,1)S(1)}, u32[]{:S(2)}, u32[]{:S(2)}) collective-permute-start(bf16[2,64,3,64]{3,1,2,0:T(8,128)(2,1)S(1)} %copy.200), channel_id=1, source_target_pairs={{30,0},{0,2},{2,4},{4,6},{6,8},{8,10},{10,12},{12,14},{14,16},{16,... | collective-permute-start | bytes 147464 | tf_op jit(solution)/shard_map/while/body/eval_jaxpr/ppermute | solution.py:19
  317.8 14.1 %collective-permute-start = (bf16[2,64,3,64]{3,1,2,0:T(8,128)(2,1)S(1)}, bf16[2,64,3,64]{3,1,2,0:T(8,128)(2,1)S(1)}, u32[]{:S(2)}, u32[]{:S(2)}) collective-permute-start(bf16[2,64,3,64]{3,1,2,0:T(8,128)(2,1)S(1)} %copy.200), channel_id=1, source_target_pairs={{30,0},{0,2},{2,4},{4,6},{6,8},{8,10},{10,12},{12,14},{14,16},{16,... | collective-permute-start | bytes 147464 | tf_op jit(solution)/shard_map/while/body/eval_jaxpr/ppermute | solution.py:19
  331.9 13.9 %collective-permute-start = (bf16[2,64,3,64]{3,1,2,0:T(8,128)(2,1)S(1)}, bf16[2,64,3,64]{3,1,2,0:T(8,128)(2,1)S(1)}, u32[]{:S(2)}, u32[]{:S(2)}) collective-permute-start(bf16[2,64,3,64]{3,1,2,0:T(8,128)(2,1)S(1)} %copy.200), channel_id=1, source_target_pairs={{30,0},{0,2},{2,4},{4,6},{6,8},{8,10},{10,12},{12,14},{14,16},{16,... | collective-permute-start | bytes 147464 | tf_op jit(solution)/shard_map/while/body/eval_jaxpr/ppermute | solution.py:19
  333.6 12.3 %collective-permute-start.1 = (bf16[2,64,3,64]{3,1,2,0:T(8,128)(2,1)S(1)}, bf16[2,64,3,64]{3,1,2,0:T(8,128)(2,1)S(1)}, u32[]{:S(2)}, u32[]{:S(2)}) collective-permute-start(bf16[2,64,3,64]{3,1,2,0:T(8,128)(2,1)S(1)} %copy.201), channel_id=1, source_target_pairs={{30,0},{0,2},{2,4},{4,6},{6,8},{8,10},{10,12},{12,14},{14,16},{16,... | collective-permute-start | bytes 147464 | tf_op jit(solution)/shard_map/while/body/eval_jaxpr/ppermute | solution.py:19
  345.9 13.8 %collective-permute-start = (bf16[2,64,3,64]{3,1,2,0:T(8,128)(2,1)S(1)}, bf16[2,64,3,64]{3,1,2,0:T(8,128)(2,1)S(1)}, u32[]{:S(2)}, u32[]{:S(2)}) collective-permute-start(bf16[2,64,3,64]{3,1,2,0:T(8,128)(2,1)S(1)} %copy.200), channel_id=1, source_target_pairs={{30,0},{0,2},{2,4},{4,6},{6,8},{8,10},{10,12},{12,14},{14,16},{16,... | collective-permute-start | bytes 147464 | tf_op jit(solution)/shard_map/while/body/eval_jaxpr/ppermute | solution.py:19
  347.6 12.2 %collective-permute-start.1 = (bf16[2,64,3,64]{3,1,2,0:T(8,128)(2,1)S(1)}, bf16[2,64,3,64]{3,1,2,0:T(8,128)(2,1)S(1)}, u32[]{:S(2)}, u32[]{:S(2)}) collective-permute-start(bf16[2,64,3,64]{3,1,2,0:T(8,128)(2,1)S(1)} %copy.201), channel_id=1, source_target_pairs={{30,0},{0,2},{2,4},{4,6},{6,8},{8,10},{10,12},{12,14},{14,16},{16,... | collective-permute-start | bytes 147464 | tf_op jit(solution)/shard_map/while/body/eval_jaxpr/ppermute | solution.py:19
  366.0 38.3 %reduce-scatter.10.cloned.1.call-start = ((), (), s32[]{:S(2)}) async-start(), calls=%async_computation.11 | async-start | bytes 442368 | tf_op jit(solution)/shard_map/reduce_scatter | solution.py:316
  369.7 46.1 %reduce-scatter.14.cloned.1.call-start = ((), (), s32[]{:S(2)}) async-start(), calls=%async_computation.13 | async-start | bytes 1105920 | tf_op jit(solution)/shard_map/reduce_scatter | solution.py:322
  371.0 57.0 %reduce-scatter.8.cloned.1.call-start = ((), (), s32[]{:S(2)}) async-start(), calls=%async_computation.10 | async-start | bytes 1105920 | tf_op jit(solution)/shard_map/reduce_scatter | solution.py:313
  373.6 67.8 %reduce-scatter.18.cloned.1.call-start = ((), (), s32[]{:S(2)}) async-start(), calls=%async_computation.15 | async-start | bytes 2654208 | tf_op jit(solution)/shard_map/reduce_scatter | solution.py:331
  375.5 79.3 %reduce-scatter.16.cloned.1.call-start = ((), (), s32[]{:S(2)}) async-start(), calls=%async_computation.14 | async-start | bytes 2654208 | tf_op jit(solution)/shard_map/reduce_scatter | solution.py:328
  377.4 90.6 %reduce-scatter.20.cloned.1.call-start = ((), (), s32[]{:S(2)}) async-start(), calls=%async_computation.16 | async-start | bytes 2654208 | tf_op jit(solution)/shard_map/reduce_scatter | solution.py:334
  379.4 256.8 %all-reduce.10.cloned.1.call-start = ((), (), s32[]{:S(2)}) async-start(), calls=%async_computation.17 | async-start | bytes 7372800 | tf_op jit(solution)/shard_map/psum | solution.py:342
  (92 other events, 769.0 us)
Sparse Core Ops, SparseCore 0:
  9.6 11.7 all-gather.3
  23.0 11.2 all-gather.5
  35.8 11.2 all-gather.7
  366.1 27.1 reduce-scatter.11
  395.4 8.8 reduce-scatter.9
  406.4 9.3 reduce-scatter.13
  418.6 9.3 reduce-scatter.7
  430.9 10.4 reduce-scatter.17
  444.3 10.4 reduce-scatter.15
  457.5 10.4 reduce-scatter.19
  475.5 160.5 all-reduce.9
where the time goes:
time: 657 us; the launch traced here: 651 us
  waiting for transfers between devices  274 us (42%)
  blocking collectives  145 us (22%)
  starting transfers between devices  91.8 us (14%)
  matrix products  68.4 us (10%)
  other arithmetic  44.1 us (7%)
  between operations  16.1 us (2%)
  local copies, waits for them, and re-layouts  10.6 us (2%)
    psum x1, waiting for transfers between devices, local(): lax.psum(owned_grads[0].astype(jnp.bfloat16), 'ctx').astype(jnp.float32)  130 us
    ppermute x62, starting transfers between devices, shifted(): return lax.ppermute(block, axis, route)  91.1 us
    ppermute x62, waiting for transfers between devices, shifted(): return lax.ppermute(block, axis, route)  53.1 us
    all_gather x1, blocking collectives, local(): value_part = lax.all_gather(value_rows, 'ctx', axis=1, tiled=True)  47 us
    all_gather x1, blocking collectives, local(): key_part = lax.all_gather(key_rows, 'ctx', axis=1, tiled=True)  42.7 us
    psum x1, blocking collectives, local(): lax.psum(owned_grads[4].astype(jnp.bfloat16), 'ctx').astype(jnp.float32)  28.6 us
    dot_general x16, matrix products, block_grads(): jnp.einsum('sqkgd,snkd->skgqn', queries, key_part, preferred_element_type...  17 us
    reduce_scatter x1, waiting for transfers between devices, local(): lax.psum_scatter(grad_wvalue.astype(jnp.bfloat16), 'fsdp', scatter_dimens...  13.7 us
  transfers between devices with their start and end apart: 73, of which 40 were waited for; matrix products, arithmetic and copies ran while one was open for 16% of the time, Pallas kernels for 0%

commit v1 on v0

v1 whole, which is shorter than its diff:
```python
import functools

import jax
import jax.numpy as jnp
from jax import lax
from jax.experimental import pallas as pl
from jax.experimental.pallas import tpu as pltpu
from jax.sharding import PartitionSpec as P

HEADS = 9
KV_HEADS = 3
HEAD_DIM = 64
LANES = 128
CHUNKS = 3
EXTRA_ROWS = 16

epsilon = 1e-05
theta_base = 100000.0
masked_value = -1e30
MESH = pl.DeviceIdType.MESH

ORDERS = ((2, 1, 0), (1, 0, 2), (0, 2, 1))


def ctx_dims(count):
    return (count // 4, 2, 2)


class Links:
    def __init__(self, send_sem, recv_sem, dims):
        self.send_sem = send_sem
        self.recv_sem = recv_sem
        self.dims = dims
        self.me = lax.axis_index("ctx")
        self.strides = (dims[1] * dims[2], dims[2], 1)
        self.coords = tuple(
            lax.rem(lax.div(self.me, stride), size) for stride, size in zip(self.strides, dims)
        )
        self.used = 0
        self.copies = []

    def peer(self, axis, step):
        size = self.dims[axis]
        other = lax.rem(self.coords[axis] + step, size)
        return other, self.me + (other - self.coords[axis]) * self.strides[axis]

    def send(self, source, target, device_id):
        copy = pltpu.make_async_remote_copy(
            src_ref=source,
            dst_ref=target,
            send_sem=self.send_sem.at[self.used],
            recv_sem=self.recv_sem.at[self.used],
            device_id=device_id,
            device_id_type=MESH,
        )
        copy.start()
        self.used += 1
        self.copies.append(copy)
        return copy

    def finish(self):
        for copy in self.copies:
            copy.wait_send()


def greet(links, fsdp_count):
    barrier = pltpu.get_barrier_semaphore()
    total = 0
    for axis in range(3):
        for step in range(1, links.dims[axis]):
            _, device = links.peer(axis, step)
            pl.semaphore_signal(barrier, inc=1, device_id={"ctx": device}, device_id_type=MESH)
            total += 1
    mine = lax.axis_index("fsdp")
    for step in range(1, fsdp_count):
        device = lax.rem(mine + step, fsdp_count)
        pl.semaphore_signal(barrier, inc=1, device_id={"fsdp": device}, device_id_type=MESH)
        total += 1
    pl.semaphore_wait(barrier, total)


def pick(choices):
    return tuple(slice(None) if choice is None else choice for choice in choices)


def add_blocks(target, parts, shape):
    total = 1
    for size in shape:
        total *= size
    sizes = shape

    def split(index):
        places = []
        for size in reversed(sizes):
            places.append(lax.rem(index, size))
            index = lax.div(index, size)
        return tuple(reversed(places))

    def body(index, carry):
        places = split(index)
        value = parts[0](places).astype(jnp.float32)
        for part in parts[1:]:
            value = value + part(places).astype(jnp.float32)
        target(places, value)
        return carry

    if total == 1:
        body(0, 0)
    else:
        lax.fori_loop(0, total, body, 0)


def scatter_begin(links, order, stage, source, slots):
    axis = order[stage]
    left = [a for a in range(3) if a not in order[:stage]]
    copies = []
    for step in range(1, links.dims[axis]):
        other, device = links.peer(axis, step)
        index = pick([other if a == axis else None for a in left])
        part = source.at[index] if isinstance(index, tuple) else source
        copies.append(links.send(part, slots.at[step - 1], {"ctx": device}))
    return copies


def scatter_end(links, order, stage, copies, source, slots, store):
    axis = order[stage]
    left = [a for a in range(3) if a not in order[:stage]]
    keep = [a for a in left if a != axis]
    for copy in copies:
        copy.wait_recv()

    def own(places):
        where = dict(zip(keep, places))
        where[axis] = links.coords[axis]
        return source[tuple(where[a] for a in left)]

    def arrived(step):
        return lambda places: slots[(step, *places)]

    parts = [own] + [arrived(step) for step in range(links.dims[axis] - 1)]
    add_blocks(store, parts, tuple(links.dims[a] for a in keep))


def gather_begin(links, order, stage, held):
    axis = order[stage]
    whole = order[stage + 1 :]
    index = pick([None if a in whole else links.coords[a] for a in range(3)])
    copies = []
    for step in range(1, links.dims[axis]):
        _, device = links.peer(axis, step)
        copies.append(links.send(held.at[index], held.at[index], {"ctx": device}))
    return copies


def stage_shapes(dims, order, tail):
    slots, sums = [], []
    for stage in range(3):
        axis = order[stage]
        keep = tuple(dims[a] for a in range(3) if a not in order[: stage + 1])
        slots.append((dims[axis] - 1, *keep, *tail))
        if stage < 2:
            sums.append((*keep, *tail))
    return slots, sums


def copies_needed(dims):
    return sum(size - 1 for size in dims)


def run_scatter(links, sources, slots, sums, finals, ready=None):
    pending = []
    for chunk in range(CHUNKS):
        if ready is not None:
            ready(chunk)
        pending.append(scatter_begin(links, ORDERS[chunk], 0, sources[chunk], slots[chunk][0]))
    current = list(sources)
    for stage in range(3):
        for chunk in range(CHUNKS):
            order = ORDERS[chunk]
            if stage < 2:
                target = sums[chunk][stage]

                def store(places, value, target=target):
                    if places:
                        target[places] = value.astype(target.dtype)
                    else:
                        target[...] = value.astype(target.dtype)
            else:
                store = finals[chunk]
            scatter_end(
                links, order, stage, pending[chunk], current[chunk], slots[chunk][stage], store
            )
            if stage < 2:
                current[chunk] = sums[chunk][stage]
                pending[chunk] = scatter_begin(
                    links, order, stage + 1, current[chunk], slots[chunk][stage + 1]
                )


def run_gather(links, helds):
    pending = [None] * CHUNKS
    for stage in (2, 1, 0):
        for chunk in range(CHUNKS):
            if pending[chunk] is not None:
                for copy in pending[chunk]:
                    copy.wait_recv()
            pending[chunk] = gather_begin(links, ORDERS[chunk], stage, helds[chunk])
    for chunk in range(CHUNKS):
        for copy in pending[chunk]:
            copy.wait_recv()


def gather_weights_begin(links, fsdp_count, shards, fulls, local_sem):
    mine = lax.axis_index("fsdp")
    copies, own = [], []
    for place, (shard, full) in enumerate(zip(shards, fulls)):
        for step in range(1, fsdp_count):
            device = lax.rem(mine + step, fsdp_count)
            copies.append(links.send(shard, full.at[mine], {"fsdp": device}))
        copy = pltpu.make_async_copy(shard, full.at[mine], local_sem.at[place])
        copy.start()
        own.append(copy)
    return copies, own


def weights_kernel(count, fsdp_count, dims, *refs):
    shards, fulls = refs[:count], refs[count : 2 * count]
    send_sem, recv_sem, local_sem = refs[2 * count :]
    links = Links(send_sem, recv_sem, dims)
    barrier = pltpu.get_barrier_semaphore()
    mine = lax.axis_index("fsdp")
    for step in range(1, fsdp_count):
        device = lax.rem(mine + step, fsdp_count)
        pl.semaphore_signal(barrier, inc=1, device_id={"fsdp": device}, device_id_type=MESH)
    pl.semaphore_wait(barrier, fsdp_count - 1)
    copies, own = gather_weights_begin(links, fsdp_count, shards, fulls, local_sem)
    for copy in own:
        copy.wait()
    for copy in copies:
        copy.wait_recv()
    links.finish()


def gather_weights(shards, fsdp_count, dims, collective_id):
    count = len(shards)
    total = count * max(fsdp_count - 1, 1)
    fulls = pl.pallas_call(
        functools.partial(weights_kernel, count, fsdp_count, dims),
        out_shape=[jax.ShapeDtypeStruct((fsdp_count, *s.shape), s.dtype) for s in shards],
        in_specs=[pl.BlockSpec(memory_space=pl.ANY)] * count,
        out_specs=[pl.BlockSpec(memory_space=pl.ANY)] * count,
        scratch_shapes=[
            pltpu.SemaphoreType.DMA((total,)),
            pltpu.SemaphoreType.DMA((total,)),
            pltpu.SemaphoreType.DMA((count,)),
        ],
        compiler_params=pltpu.CompilerParams(collective_id=collective_id, has_side_effects=True),
        name="gather_weights",
    )(*shards)
    return [full.reshape(-1, full.shape[-1]) for full in fulls]


def kv_gather_kernel(count, fsdp_count, dims, *refs):
    kv, shards = refs[0], refs[1 : 1 + count]
    held, fulls = refs[1 + count], refs[2 + count : 2 + 2 * count]
    send_sem, recv_sem, local_sem = refs[2 + 2 * count :]
    links = Links(send_sem, recv_sem, dims)
    greet(links, fsdp_count)
    for chunk in range(CHUNKS):
        held[(chunk, *links.coords)] = kv[chunk]
    copies, own = gather_weights_begin(links, fsdp_count, shards, fulls, local_sem)
    run_gather(links, [held.at[chunk] for chunk in range(CHUNKS)])
    for copy in own:
        copy.wait()
    for copy in copies:
        copy.wait_recv()
    links.finish()


def gather_kv(kv, shards, fsdp_count, dims, collective_id):
    count = len(shards)
    total = count * (fsdp_count - 1) + CHUNKS * copies_needed(dims)
    results = pl.pallas_call(
        functools.partial(kv_gather_kernel, count, fsdp_count, dims),
        out_shape=[jax.ShapeDtypeStruct((CHUNKS, *dims, *kv.shape[1:]), kv.dtype)]
        + [jax.ShapeDtypeStruct((fsdp_count, *s.shape), s.dtype) for s in shards],
        in_specs=[pl.BlockSpec(memory_space=pltpu.VMEM)]
        + [pl.BlockSpec(memory_space=pl.ANY)] * count,
        out_specs=[pl.BlockSpec(memory_space=pltpu.VMEM)]
        + [pl.BlockSpec(memory_space=pl.ANY)] * count,
        scratch_shapes=[
            pltpu.SemaphoreType.DMA((total,)),
            pltpu.SemaphoreType.DMA((total,)),
            pltpu.SemaphoreType.DMA((count,)),
        ],
        compiler_params=pltpu.CompilerParams(
            collective_id=collective_id, has_side_effects=True, vmem_limit_bytes=32 << 20
        ),
        name="gather_kv",
    )(kv, *shards)
    return results[0], [full.reshape(-1, full.shape[-1]) for full in results[1:]]


def kv_scatter_kernel(dims, *refs):
    parts, out = refs[0], refs[1]
    refs = refs[2:]
    slots = [refs[5 * c : 5 * c + 3] for c in range(CHUNKS)]
    sums = [refs[5 * c + 3 : 5 * c + 5] for c in range(CHUNKS)]
    send_sem, recv_sem = refs[5 * CHUNKS :]
    links = Links(send_sem, recv_sem, dims)
    greet(links, 1)

    def final(chunk):
        def store(places, value):
            out[chunk] = value

        return store

    run_scatter(
        links,
        [parts.at[chunk] for chunk in range(CHUNKS)],
        slots,
        sums,
        [final(chunk) for chunk in range(CHUNKS)],
    )
    links.finish()


def scatter_scratch(dims, tail):
    scratch = []
    for order in ORDERS:
        slots, sums = stage_shapes(dims, order, tail)
        scratch += [pltpu.VMEM(shape, jnp.bfloat16) for shape in slots + sums]
    return scratch


def scatter_kv(parts, dims, collective_id):
    tail = parts.shape[-2:]
    total = CHUNKS * copies_needed(dims)
    return pl.pallas_call(
        functools.partial(kv_scatter_kernel, dims),
        out_shape=jax.ShapeDtypeStruct((CHUNKS, *tail), jnp.float32),
        in_specs=[pl.BlockSpec(memory_space=pltpu.VMEM)],
        out_specs=pl.BlockSpec(memory_space=pltpu.VMEM),
        scratch_shapes=scatter_scratch(dims, tail)
        + [pltpu.SemaphoreType.DMA((total,)), pltpu.SemaphoreType.DMA((total,))],
        compiler_params=pltpu.CompilerParams(
            collective_id=collective_id, has_side_effects=True, vmem_limit_bytes=32 << 20
        ),
        name="scatter_kv",
    )(parts)


def sum_grads_kernel(fsdp_count, dims, *refs):
    grads, out = refs[0], refs[1]
    arrived, current = refs[2], refs[3]
    refs = refs[4:]
    slots = [refs[5 * c : 5 * c + 3] for c in range(CHUNKS)]
    sums = [refs[5 * c + 3 : 5 * c + 5] for c in range(CHUNKS)]
    send_sem, recv_sem = refs[5 * CHUNKS :]
    links = Links(send_sem, recv_sem, dims)
    greet(links, fsdp_count)
    mine = lax.axis_index("fsdp")
    first = []
    for chunk in range(CHUNKS):
        first.append([])
        for step in range(1, fsdp_count):
            device = lax.rem(mine + step, fsdp_count)
            first[chunk].append(
                links.send(
                    grads.at[device, chunk], arrived.at[step - 1, chunk], {"fsdp": device}
                )
            )

    def ready(chunk):
        for copy in first[chunk]:
            copy.wait_recv()

        def store(places, value):
            current[(chunk, *places)] = value.astype(current.dtype)

        parts = [lambda places: grads[(mine, chunk, *places)]]
        for step in range(fsdp_count - 1):
            parts.append(lambda places, step=step: arrived[(step, chunk, *places)])
        add_blocks(store, parts, dims)

    def final(chunk):
        def store(places, value):
            out[(chunk, *links.coords)] = value.astype(out.dtype)

        return store

    run_scatter(
        links,
        [current.at[chunk] for chunk in range(CHUNKS)],
        slots,
        sums,
        [final(chunk) for chunk in range(CHUNKS)],
        ready,
    )
    run_gather(links, [out.at[chunk] for chunk in range(CHUNKS)])
    links.finish()


def sum_grads(grads, fsdp_count, dims, collective_id):
    tail = grads.shape[-2:]
    total = CHUNKS * (2 * copies_needed(dims) + fsdp_count - 1)
    return pl.pallas_call(
        functools.partial(sum_grads_kernel, fsdp_count, dims),
        out_shape=jax.ShapeDtypeStruct((CHUNKS, *dims, *tail), grads.dtype),
        in_specs=[pl.BlockSpec(memory_space=pltpu.VMEM)],
        out_specs=pl.BlockSpec(memory_space=pltpu.VMEM),
        scratch_shapes=[
            pltpu.VMEM((max(fsdp_count - 1, 1), CHUNKS, *dims, *tail), grads.dtype),
            pltpu.VMEM((CHUNKS, *dims, *tail), grads.dtype),
        ]
        + scatter_scratch(dims, tail)
        + [pltpu.SemaphoreType.DMA((total,)), pltpu.SemaphoreType.DMA((total,))],
        compiler_params=pltpu.CompilerParams(
            collective_id=collective_id, has_side_effects=True, vmem_limit_bytes=48 << 20
        ),
        name="sum_grads",
    )(grads)


def make_tables(positions):
    half_dim = HEAD_DIM // 2
    frequency = theta_base ** (-2.0 * jnp.arange(half_dim, dtype=jnp.float32) / HEAD_DIM)
    angles = positions.astype(jnp.float32)[:, None] * frequency[None, :]
    return (jnp.cos(angles), jnp.sin(angles))


def rotate(values, cosine, sine):
    half_dim = values.shape[-1] // 2
    first_half = values[..., :half_dim]
    second_half = values[..., half_dim:]
    cos_rows = cosine[:, None, :]
    sin_rows = sine[:, None, :]
    return jnp.concatenate(
        [
            first_half * cos_rows - second_half * sin_rows,
            second_half * cos_rows + first_half * sin_rows,
        ],
        axis=-1,
    )


def rotate_back(grads, cosine, sine):
    half_dim = grads.shape[-1] // 2
    first_half = grads[..., :half_dim]
    second_half = grads[..., half_dim:]
    cos_rows = cosine[:, None, :]
    sin_rows = sine[:, None, :]
    return jnp.concatenate(
        [
            first_half * cos_rows + second_half * sin_rows,
            second_half * cos_rows - first_half * sin_rows,
        ],
        axis=-1,
    )


def slot_positions(block_of_slot, offset, count_rows, half_len):
    row_ids = offset + jnp.arange(count_rows, dtype=jnp.int32)
    slot_ids = row_ids // half_len
    slot_match = slot_ids[:, None] == jnp.arange(block_of_slot.shape[0], dtype=jnp.int32)[None, :]
    owners = jnp.sum(jnp.where(slot_match, block_of_slot[None, :], 0), axis=1)
    return owners * half_len + row_ids % half_len


def norm_forward(values, gain_vec):
    inverse = lax.rsqrt(jnp.mean(values * values, axis=-1, keepdims=True) + epsilon)
    scaled = values * inverse
    return (scaled * gain_vec, scaled, inverse)


def norm_backward(grad_output, gain_vec, scaled, inverse):
    grad_scaled = grad_output * gain_vec
    grad_input = inverse * (
        grad_scaled - scaled * jnp.mean(grad_scaled * scaled, axis=-1, keepdims=True)
    )
    grad_gain = jnp.sum(grad_output * scaled, axis=0)
    return (grad_input, grad_gain)


def local(
    x_in,
    w_query,
    w_key,
    w_value,
    w_out,
    attn_gain,
    w_gate,
    w_up,
    w_down,
    mlp_gain,
    block_of_slot,
    out_grad,
):
    fsdp_count = lax.axis_size("fsdp")
    dims = ctx_dims(lax.axis_size("ctx"))
    full_query, full_key, full_value, gain_attn = gather_weights(
        [w_query, w_key, w_value, attn_gain.reshape(1, -1)], fsdp_count, dims, 0
    )
    gain_attn = gain_attn.reshape(-1)
    gain_attn_f = gain_attn.astype(jnp.float32)
    seq_count, tok_count, model_width = x_in.shape
    group_size = HEADS // KV_HEADS
    half_len = tok_count // 2
    rows_all = seq_count * tok_count
    ctx_count = lax.axis_size("ctx")
    score_scale = HEAD_DIM ** (-0.5)
    my_offset = lax.axis_index("ctx") * tok_count
    query_pos = slot_positions(block_of_slot, my_offset, tok_count, half_len)
    cosine, sine = make_tables(query_pos)
    inputs = x_in.astype(jnp.float32).reshape(rows_all, model_width)
    normed_f, scaled_one, inverse_one = norm_forward(inputs, gain_attn_f)
    normed = normed_f.astype(jnp.bfloat16)
    query_f = jnp.dot(normed, full_query, preferred_element_type=jnp.float32).reshape(
        seq_count, tok_count, HEADS, HEAD_DIM
    )
    queries = (
        rotate(query_f, cosine, sine)
        .astype(jnp.bfloat16)
        .reshape(seq_count, tok_count, KV_HEADS, group_size, HEAD_DIM)
    )
    key_f = jnp.dot(normed, full_key, preferred_element_type=jnp.float32).reshape(
        seq_count, tok_count, KV_HEADS, HEAD_DIM
    )
    key_rows = rotate(key_f, cosine, sine).astype(jnp.bfloat16)
    value_rows = (
        jnp.dot(normed, full_value, preferred_element_type=jnp.float32)
        .astype(jnp.bfloat16)
        .reshape(seq_count, tok_count, KV_HEADS, HEAD_DIM)
    )
    kv_rows = (
        jnp.concatenate([key_rows, value_rows], axis=-1)
        .reshape(rows_all, KV_HEADS, 2 * HEAD_DIM)
        .transpose(1, 0, 2)
    )
    kv_all, (full_out, full_gate, full_up, full_down, gain_mlp) = gather_kv(
        kv_rows, [w_out, w_gate, w_up, w_down, mlp_gain.reshape(1, -1)], fsdp_count, dims, 1
    )
    gain_mlp_f = gain_mlp.reshape(-1).astype(jnp.float32)
    kv_all = (
        kv_all.reshape(KV_HEADS, ctx_count, seq_count, tok_count, 2 * HEAD_DIM)
        .transpose(2, 0, 1, 3, 4)
        .reshape(seq_count, KV_HEADS, ctx_count * tok_count, 2 * HEAD_DIM)
    )
    key_all = kv_all[..., :HEAD_DIM]
    value_all = kv_all[..., HEAD_DIM:]
    queries = queries.transpose(0, 2, 3, 1, 4).reshape(
        seq_count, KV_HEADS, group_size * tok_count, HEAD_DIM
    )
    key_pos = slot_positions(block_of_slot, jnp.int32(0), ctx_count * tok_count, half_len)
    visible = jnp.tile(query_pos, group_size)[:, None] >= key_pos[None, :]
    scores = (
        jnp.einsum("skqd,sknd->skqn", queries, key_all, preferred_element_type=jnp.float32)
        * score_scale
    )
    scores = jnp.where(visible, scores, masked_value)
    top = jnp.max(scores, axis=-1, keepdims=True)
    weights = jnp.where(visible, jnp.exp(scores - top), 0.0)
    weights = weights / jnp.sum(weights, axis=-1, keepdims=True)
    weights_low = weights.astype(jnp.bfloat16)
    attended_f = jnp.einsum(
        "skqn,sknd->skqd", weights_low, value_all, preferred_element_type=jnp.float32
    )
    attended = (
        attended_f.astype(jnp.bfloat16)
        .reshape(seq_count, HEADS, tok_count, HEAD_DIM)
        .transpose(0, 2, 1, 3)
        .reshape(rows_all, model_width)
    )
    hidden_state = inputs + jnp.dot(attended, full_out, preferred_element_type=jnp.float32)
    normed_two_f, scaled_two, inverse_two = norm_forward(hidden_state, gain_mlp_f)
    normed_two = normed_two_f.astype(jnp.bfloat16)
    gate_vals = jnp.dot(normed_two, full_gate, preferred_element_type=jnp.float32)
    up_vals = jnp.dot(normed_two, full_up, preferred_element_type=jnp.float32)
    sigmoid_gate = jax.nn.sigmoid(gate_vals)
    activated = gate_vals * sigmoid_gate
    inner_rows = (activated * up_vals).astype(jnp.bfloat16)
    result = hidden_state + jnp.dot(inner_rows, full_down, preferred_element_type=jnp.float32)
    y_out = result.reshape(seq_count, tok_count, model_width).astype(jnp.bfloat16)
    grad_top = out_grad.reshape(rows_all, model_width)
    grad_residual = grad_top.astype(jnp.float32)
    grad_wdown = jnp.einsum("rf,rd->fd", inner_rows, grad_top, preferred_element_type=jnp.float32)
    grad_inner = jnp.einsum("rd,fd->rf", grad_top, full_down, preferred_element_type=jnp.float32)
    grad_gate = (
        grad_inner * up_vals * sigmoid_gate * (1.0 + gate_vals * (1.0 - sigmoid_gate))
    ).astype(jnp.bfloat16)
    grad_up = (grad_inner * activated).astype(jnp.bfloat16)
    grad_wgate = jnp.einsum("rd,rf->df", normed_two, grad_gate, preferred_element_type=jnp.float32)
    grad_wup = jnp.einsum("rd,rf->df", normed_two, grad_up, preferred_element_type=jnp.float32)
    grad_normed_two = jnp.einsum(
        "rf,df->rd", grad_gate, full_gate, preferred_element_type=jnp.float32
    ) + jnp.einsum("rf,df->rd", grad_up, full_up, preferred_element_type=jnp.float32)
    grad_hidden_norm, grad_gain_mlp = norm_backward(
        grad_normed_two, gain_mlp_f, scaled_two, inverse_two
    )
    grad_hidden = grad_residual + grad_hidden_norm
    grad_branch = grad_hidden.astype(jnp.bfloat16)
    grad_wout = jnp.einsum("ri,rj->ij", attended, grad_branch, preferred_element_type=jnp.float32)
    grad_attended = jnp.einsum(
        "rj,ij->ri", grad_branch, full_out, preferred_element_type=jnp.float32
    ).astype(jnp.bfloat16)
    grad_heads = (
        grad_attended.reshape(seq_count, tok_count, HEADS, HEAD_DIM)
        .transpose(0, 2, 1, 3)
        .reshape(seq_count, KV_HEADS, group_size * tok_count, HEAD_DIM)
    )
    row_delta = jnp.sum(grad_heads.astype(jnp.float32) * attended_f, axis=-1, keepdims=True)
    grad_value_part = jnp.einsum(
        "skqn,skqd->sknd", weights_low, grad_heads, preferred_element_type=jnp.float32
    )
    grad_weights = jnp.einsum(
        "skqd,sknd->skqn", grad_heads, value_all, preferred_element_type=jnp.float32
    )
    grad_scores = (weights * (grad_weights - row_delta)).astype(jnp.bfloat16)
    grad_query = jnp.einsum(
        "skqn,sknd->skqd", grad_scores, key_all, preferred_element_type=jnp.float32
    )
    grad_key_part = (
        jnp.einsum("skqn,skqd->sknd", grad_scores, queries, preferred_element_type=jnp.float32)
        * score_scale
    )
    grad_kv_part = (
        jnp.concatenate([grad_key_part, grad_value_part], axis=-1)
        .astype(jnp.bfloat16)
        .reshape(seq_count, KV_HEADS, ctx_count, tok_count, 2 * HEAD_DIM)
        .transpose(1, 2, 0, 3, 4)
        .reshape(KV_HEADS, *dims, rows_all, 2 * HEAD_DIM)
    )
    grad_kv = (
        scatter_kv(grad_kv_part, dims, 2)
        .transpose(1, 0, 2)
        .reshape(seq_count, tok_count, KV_HEADS, 2 * HEAD_DIM)
    )
    grad_key = grad_kv[..., :HEAD_DIM]
    grad_value = grad_kv[..., HEAD_DIM:]
    grad_query_rows = (
        (grad_query * score_scale)
        .reshape(seq_count, HEADS, tok_count, HEAD_DIM)
        .transpose(0, 2, 1, 3)
    )
    grad_query_low = (
        rotate_back(grad_query_rows, cosine, sine)
        .astype(jnp.bfloat16)
        .reshape(rows_all, model_width)
    )
    grad_key_low = (
        rotate_back(grad_key, cosine, sine)
        .astype(jnp.bfloat16)
        .reshape(rows_all, KV_HEADS * HEAD_DIM)
    )
    grad_value_low = grad_value.astype(jnp.bfloat16).reshape(rows_all, KV_HEADS * HEAD_DIM)
    grad_wquery = jnp.einsum(
        "rd,re->de", normed, grad_query_low, preferred_element_type=jnp.float32
    )
    grad_wkey = jnp.einsum("rd,re->de", normed, grad_key_low, preferred_element_type=jnp.float32)
    grad_wvalue = jnp.einsum(
        "rd,re->de", normed, grad_value_low, preferred_element_type=jnp.float32
    )
    grad_normed = jnp.einsum(
        "re,de->rd", grad_query_low, full_query, preferred_element_type=jnp.float32
    )
    grad_normed = grad_normed + jnp.einsum(
        "re,de->rd", grad_key_low, full_key, preferred_element_type=jnp.float32
    )
    grad_normed = grad_normed + jnp.einsum(
        "re,de->rd", grad_value_low, full_value, preferred_element_type=jnp.float32
    )
    grad_input_norm, grad_gain_attn = norm_backward(
        grad_normed, gain_attn_f, scaled_one, inverse_one
    )
    x_grad = (
        (grad_hidden + grad_input_norm)
        .astype(jnp.bfloat16)
        .reshape(seq_count, tok_count, model_width)
    )
    shard_rows = model_width // fsdp_count
    wide = [grad_wquery, grad_wkey, grad_wvalue, grad_wout, grad_wgate, grad_wup]
    widths = [grad.shape[1] for grad in wide]
    columns = jnp.concatenate([grad.astype(jnp.bfloat16) for grad in wide], axis=1)
    wide_tiles = columns.shape[1] // LANES
    columns = columns.reshape(fsdp_count, shard_rows, wide_tiles, LANES).transpose(0, 2, 1, 3)
    hidden = grad_wdown.shape[0]
    half_hidden = hidden // (2 * fsdp_count)
    down_tiles = 2 * model_width // LANES
    down = (
        grad_wdown.astype(jnp.bfloat16)
        .reshape(fsdp_count, 2, half_hidden, model_width)
        .transpose(0, 2, 1, 3)
        .reshape(fsdp_count, half_hidden, down_tiles, LANES)
        .transpose(0, 2, 1, 3)
        .reshape(fsdp_count, -1, shard_rows, LANES)
    )
    tiles = jnp.concatenate([columns, down], axis=1)
    gains = (
        jnp.stack([grad_gain_attn, grad_gain_mlp])
        .astype(jnp.bfloat16)
        .reshape(2, fsdp_count, shard_rows)
        .transpose(1, 0, 2)
        .reshape(fsdp_count, 2 * shard_rows)
    )
    used_tiles = tiles.shape[1]
    tile_count = used_tiles + -used_tiles % (CHUNKS * ctx_count)
    tiles = jnp.pad(tiles, ((0, 0), (0, tile_count - used_tiles), (0, 0), (0, 0)))
    gains = jnp.pad(gains, ((0, 0), (0, EXTRA_ROWS * LANES - 2 * shard_rows)))
    gains = jnp.pad(
        gains.reshape(fsdp_count, 1, EXTRA_ROWS, LANES),
        ((0, 0), (0, tile_count - 1), (0, 0), (0, 0)),
    )
    packed = jnp.concatenate([tiles, gains], axis=2).reshape(
        fsdp_count, CHUNKS, *dims, shard_rows + EXTRA_ROWS, LANES
    )
    summed = sum_grads(packed, fsdp_count, dims, 3).reshape(
        tile_count, shard_rows + EXTRA_ROWS, LANES
    )
    gains = summed[0, shard_rows:].astype(jnp.float32).reshape(-1)
    columns = (
        summed[:wide_tiles, :shard_rows]
        .transpose(1, 0, 2)
        .reshape(shard_rows, wide_tiles * LANES)
        .astype(jnp.float32)
    )
    owned, offset = [], 0
    for width in widths:
        owned.append(columns[:, offset : offset + width])
        offset += width
    down = (
        summed[wide_tiles:used_tiles, :shard_rows]
        .reshape(down_tiles, half_hidden, LANES)
        .transpose(1, 0, 2)
        .reshape(half_hidden, 2, model_width)
        .transpose(1, 0, 2)
        .reshape(2 * half_hidden, model_width)
        .astype(jnp.float32)
    )
    return (
        y_out,
        x_grad,
        owned[0],
        owned[1],
        owned[2],
        owned[3],
        gains[:shard_rows],
        owned[4],
        owned[5],
        down,
        gains[shard_rows : 2 * shard_rows],
    )


def solution(mesh):
    placed = (
        P("fsdp", "ctx", None),
        P("fsdp", None),
        P("fsdp", None),
        P("fsdp", None),
        P("fsdp", None),
        P("fsdp"),
        P("fsdp", None),
        P("fsdp", None),
        P("fsdp", None),
        P("fsdp"),
        P(),
        P("fsdp", "ctx", None),
    )
    return jax.shard_map(
        local,
        mesh=mesh,
        in_specs=placed,
        out_specs=(
            P("fsdp", "ctx", None),
            P("fsdp", "ctx", None),
            P("fsdp", None),
            P("fsdp", None),
            P("fsdp", None),
            P("fsdp", None),
            P("fsdp"),
            P("fsdp", None),
            P("fsdp", None),
            P("fsdp", None),
            P("fsdp"),
        ),
        check_vma=False,
    )
```

time: 657 us -> 331 us (0.50)
  waiting for transfers between devices: 274 us -> 0 us
  Pallas kernels: 0 us -> 182 us
  blocking collectives: 145 us -> 0 us
  starting transfers between devices: 91.8 us -> 0 us
  local copies, waits for them, and re-layouts: 10.6 us -> 87.5 us
  matrix products: 68.4 us -> 35.1 us
  other arithmetic: 44.1 us -> 23.3 us
  between operations: 16.1 us -> 1.59 us
    pallas_call x0 -> x4, Pallas kernels: none -> 182 us  [the longest x1 111 us: sum_grads(): pl.pallas_call(functools.partial(sum_grads_kernel, fsdp_count, dims), out...]
    psum x1 -> x0, waiting for transfers between devices: 130 us -> none  [local(): lax.psum(owned_grads[0].astype(jnp.bfloat16), 'ctx').astype(jnp.float32)]
    all_gather x6 -> x0, blocking collectives: 111 us -> none  [the longest x1 47 us: local(): value_part = lax.all_gather(value_rows, 'ctx', axis=1, tiled=True)]
    ppermute x62 -> x0, starting transfers between devices: 91.1 us -> none  [shifted(): return lax.ppermute(block, axis, route)]
    reduce_scatter x7 -> x0, waiting for transfers between devices: 88.3 us -> none  [the longest x1 13.7 us: local(): lax.psum_scatter(grad_wvalue.astype(jnp.bfloat16), 'fsdp', scatter_dimens...]
    ppermute x62 -> x0, waiting for transfers between devices: 53.1 us -> none  [shifted(): return lax.ppermute(block, axis, route)]
    dot_general x82 -> x6, matrix products: 42.4 us -> 12.3 us  [the longest x1 3.22 us: local(): jnp.einsum('skqd,sknd->skqn', grad_heads, value_all, preferred_element_ty...]
    psum x1 -> x0, blocking collectives: 28.6 us -> none  [local(): lax.psum(owned_grads[4].astype(jnp.bfloat16), 'ctx').astype(jnp.float32)]
  transfers between devices with their start and end apart: 73 -> 0, of which waited for: 40 -> 0; matrix products, arithmetic and copies ran while one was open for 16% -> 0% of each run, Pallas kernels for 0% -> 0%
where the time goes in v1:
time: 331 us; the launch traced here: 329 us
  Pallas kernels  182 us (55%)
  local copies, waits for them, and re-layouts  87.5 us (26%)
  matrix products  35.1 us (11%)
  other arithmetic  23.3 us (7%)
    pallas_call x1, Pallas kernels, sum_grads(): pl.pallas_call(functools.partial(sum_grads_kernel, fsdp_count, dims), out...  111 us
    pallas_call x1, Pallas kernels, scatter_kv(): pl.pallas_call(functools.partial(kv_scatter_kernel, dims), out_shape=jax....  24.9 us
    pallas_call x1, Pallas kernels, gather_kv(): pl.pallas_call(functools.partial(kv_gather_kernel, count, fsdp_count, dim...  23.3 us
    pallas_call x1, Pallas kernels, gather_weights(): pl.pallas_call(functools.partial(weights_kernel, count, fsdp_count, dims)...  22 us
    unnamed x132, local copies, waits for them, and re-layouts  13.9 us
    reshape x1, local copies, waits for them, and re-layouts, local(): columns.reshape(fsdp_count, shard_rows, wide_tiles, LANES)  9.91 us
    concatenate x1, local copies, waits for them, and re-layouts, local(): jnp.concatenate([grad.astype(jnp.bfloat16) for grad in wide], axis=1)  9.54 us
    concatenate x4, local copies, waits for them, and re-layouts, local(): jnp.concatenate([grad_key_part, grad_value_part], axis=-1)  9.31 us

profile of v1, /device:TPU:27, one launch (start us, length us, event | category | flops | bytes accessed | tf_op | source)
XLA Modules:
  0.0 329.0 jit_solution(1272344703299162096)
XLA Ops:
  0.7 1.8 copy.186
  3.7 22.0 %gather_weights.1 = (bf16[2,288,576]{2,1,0:T(8,128)(2,1)}, bf16[2,288,192]{2,1,0:T(8,128)(2,1)}, bf16[2,288,192]{2,1,0:T(8,128)(2,1)}, bf16[2,1,288]{2,1,0:T(2,128)(2,1)}) custom-call(bf16[288,576]{1,0:T(8,128)(2,1)} %refs_0_.1, bf16[288,192]{1,0:T(8,128)(2,1)} %refs_1_.2, bf16[288,192]{1,0:T(8,128)(2,1)} %refs_2_.2, bf16[1,288]{1,0:T(2,128)(2,1)} %reshape.448.refs_3_), custom_call_target="tpu_custom_call" | custom-call | tf_op jit(solution)/shard_map/gather_weights/pallas_call | solution.py:247
  40.2 23.3 %gather_kv.1 = (bf16[3,4,2,2,128,128]{5,4,3,2,1,0:T(8,128)(2,1)S(1)}, bf16[2,288,576]{2,1,0:T(8,128)(2,1)S(1)}, bf16[2,288,1536]{2,1,0:T(8,128)(2,1)S(1)}, bf16[...) custom-call(bf16[3,128,128]{2,1,0:T(8,128)(2,1)S(1)} %copy-done.7, ...), custom_call_target="tpu_custom_call" | custom-call | tf_op jit(solution)/shard_map/gather_kv/pallas_call | solution.py:283
  64.7 2.9 fusion.11
  69.3 6.1 %fusion.45 = (f32[2,3,192]{2,1,0:T(4,128)S(1)}, f32[2,3,192,1024]{3,2,1,0:T(8,128)S(1)}) fusion(f32[2,3,192,1024]{3,2,1,0:T(8,128)} %fusion.11, pred[192,1024]{1,0:T(8,128)(4,1)S(1)} %broadcast_compare_fusion), kind=kOutput, calls=%fused_computation.122 | output fusion | flops 8258559 | bytes 9638400 | tf_op jit(solution)/shard_map/sub | solution.py:563
  78.0 2.3 fusion.46
  80.3 1.8 copy.184
  82.1 1.9 copy.185
  84.0 1.8 reshape.457
  85.8 2.4 multiply_reduce_fusion.6
  91.0 1.8 multiply_convert_fusion.2
  102.7 3.2 multiply_convert_fusion
  109.2 2.2 copy.194
  113.7 1.8 convert_element_type.203
  115.6 2.0 fusion.50
  119.1 1.9 concatenate.60
  121.0 2.8 copy.199
  125.3 2.6 concatenate.59
  128.0 2.0 copy.198
  129.9 2.3 pad_maximum_fusion
  132.2 24.9 %scatter_kv.1 = f32[3,128,128]{2,1,0:T(8,128)S(1)} custom-call(bf16[3,4,2,2,128,128]{5,4,3,2,1,0:T(8,128)(2,1)S(1)} %bitcast.164), custom_call_target="tpu_custom_call" | custom-call | tf_op jit(solution)/shard_map/scatter_kv/pallas_call | solution.py:340
  163.0 2.3 copy.210
  165.3 2.3 copy.211
  170.9 1.8 copy.208
  173.9 2.9 convolution_convert_fusion.2
  176.8 1.8 convolution_convert_fusion.1
  178.6 9.5 %concatenate.63 = bf16[576,4608]{1,0:T(8,128)(2,1)} concatenate(bf16[576,576]{1,0:T(8,128)(2,1)} %convolution_convert_fusion.5, bf16[576,192]{1,0:T(8,128)(2,1)S(1)} %copy-done.39, bf16[576,192]{1,0:T(8,128)(2,1)} %copy.208, bf16[576,576]{1,0:T(8,128)(2,1)} %convolution_convert_fusion.4, bf16[576,1536]{1,0:T(8,128)(2,1)} %convolution_convert_fusion.2, ...), dimensions={1} | concatenate | bytes 10616832 | tf_op jit(solution)/shard_map/concatenate | solution.py:684
  188.2 9.9 %reshape.470 = bf16[2,288,36,128]{3,2,1,0:T(8,128)(2,1)} reshape(bf16[576,4608]{1,0:T(8,128)(2,1)} %concatenate.63) | data formatting | bytes 10616832 | tf_op jit(solution)/shard_map/reshape | solution.py:686
  198.1 6.3 %fusion.2 = bf16[2,48,304,128]{3,1,2,0:T(8,128)(2,1)S(1)} fusion(bf16[2,1,16,128]{3,1,2,0:T(2,128)(2,1)S(1)} %copy-done.56, bf16[2,12,288,128]{3,1,2,0:T(8,128)(2,1)S(1)} %copy.211, bf16[2,36,288,128]{3,1,2,0:T(8,128)(2,1)} %bitcast.177), kind=kLoop, calls=%fused_computation.3 | loop fusion | flops 29884416 | bytes 14557184 | tf_op jit(solution)/shard_map/concatenate | solution.py:714
  204.4 4.9 %copy.214 = bf16[2,48,304,128]{3,2,1,0:T(8,128)(2,1)} copy(bf16[2,48,304,128]{3,1,2,0:T(8,128)(2,1)S(1)} %fusion.2) | data formatting | bytes 14942208 | tf_op jit(solution)/shard_map/concatenate | solution.py:714
  209.3 111.3 %sum_grads.1 = bf16[3,4,2,2,304,128]{5,4,3,2,1,0:T(8,128)(2,1)S(1)} custom-call(bf16[2,3,4,2,2,304,128]{6,5,4,3,2,1,0:T(8,128)(2,1)} %bitcast.172), custom_call_target="tpu_custom_call" | custom-call | tf_op jit(solution)/shard_map/sum_grads/pallas_call | solution.py:408
  324.0 2.0 fusion.40
  (229 shorter events, 58.6 us)
Async XLA Ops:
  0.6 27.4 %copy-start.36 = (bf16[2,64,576]{2,1,0:T(8,128)(2,1)S(1)}, bf16[2,64,576]{2,1,0:T(8,128)(2,1)}, u32[]{:S(2)}) copy-start(bf16[2,64,576]{2,1,0:T(8,128)(2,1)} %param.12) | copy-start | bytes 442372
  0.7 28.6 %copy-start.63 = (s32[32]{0:T(128)S(1)}, s32[32]{0:T(128)}, u32[]{:S(2)}) copy-start(s32[32]{0:T(128)} %param.22) | copy-start | bytes 388
  28.0 3.5 %copy-start.43 = (bf16[2,288,192]{2,1,0:T(8,128)(2,1)S(1)}, bf16[2,288,192]{2,1,0:T(8,128)(2,1)}, u32[]{:S(2)}) copy-start(bf16[2,288,192]{2,1,0:T(8,128)(2,1)} %get-tuple-element.24) | copy-start | bytes 663556
  28.8 3.3 copy-start.16
  28.8 3.1 copy-start.40
  30.2 3.3 %copy-start.45 = (bf16[768,576]{0,1:T(8,128)(2,1)S(1)}, bf16[768,576]{0,1:T(8,128)(2,1)}, u32[]{:S(2)}) copy-start(bf16[768,576]{0,1:T(8,128)(2,1)} %param.20) | copy-start | bytes 2654212
  31.5 3.3 %copy-start.62 = (bf16[288]{0:T(512)(128)(2,1)S(1)}, bf16[288]{0:T(512)(128)(2,1)}, u32[]{:S(2)}) copy-start(bf16[288]{0:T(512)(128)(2,1)} %param.21) | copy-start | bytes 1732
  63.5 4.2 %copy-start.1 = (bf16[2,288,576]{2,1,0:T(8,128)(2,1)}, bf16[2,288,576]{2,1,0:T(8,128)(2,1)S(1)}, u32[]{:S(2)}) copy-start(bf16[2,288,576]{2,1,0:T(8,128)(2,1)S(1)} %get-tuple-element.26) | copy-start | bytes 1990660
  63.5 4.1 %copy-start.3 = (bf16[2,768,576]{2,1,0:T(8,128)(2,1)}, bf16[2,768,576]{2,1,0:T(8,128)(2,1)S(1)}, u32[]{:S(2)}) copy-start(bf16[2,768,576]{2,1,0:T(8,128)(2,1)S(1)} %get-tuple-element.30) | copy-start | bytes 5308420
  63.6 4.0 %copy-start.9 = (bf16[3,16,2,64,128]{4,3,1,0,2:T(8,128)(2,1)}, bf16[3,16,2,64,128]{4,3,1,0,2:T(8,128)(2,1)S(1)}, u32[]{:S(2)}) copy-start(bf16[3,16,2,64,128]{4,3,1,0,2:T(8,128)(2,1)S(1)} %copy.180) | copy-start | bytes 4718596
  64.7 3.0 copy-start.61
  101.2 57.7 %copy-start.22 = (f32[128,576]{0,1:T(8,128)}, f32[128,576]{0,1:T(8,128)S(1)}, u32[]{:S(2)}) copy-start(f32[128,576]{0,1:T(8,128)S(1)} %multiply_add_fusion) | copy-start | bytes 884740
  102.1 3.8 %copy-start.30 = (bf16[2,64,9,64]{3,1,2,0:T(8,128)(2,1)}, bf16[2,64,9,64]{3,1,2,0:T(8,128)(2,1)S(1)}, u32[]{:S(2)}) copy-start(bf16[2,64,9,64]{3,1,2,0:T(8,128)(2,1)S(1)} %copy.190) | copy-start | bytes 442372
  107.3 4.2 %copy-start.53 = (f32[64,32]{0,1:T(8,128)S(1)}, f32[64,32]{0,1:T(8,128)}, u32[]{:S(2)}) copy-start(f32[64,32]{0,1:T(8,128)} %copy-done.52) | copy-start | bytes 24580
  107.3 4.2 %copy-start.55 = (f32[64,32]{0,1:T(8,128)S(1)}, f32[64,32]{0,1:T(8,128)}, u32[]{:S(2)}) copy-start(f32[64,32]{0,1:T(8,128)} %copy-done.54) | copy-start | bytes 24580
  108.2 7.4 %copy-start.27 = (bf16[2,288,576]{2,1,0:T(8,128)(2,1)S(1)}, bf16[2,288,576]{2,1,0:T(8,128)(2,1)}, u32[]{:S(2)}) copy-start(bf16[2,288,576]{2,1,0:T(8,128)(2,1)} %get-tuple-element.22) | copy-start | bytes 1990660
  109.2 8.3 %copy-start.13 = (bf16[2,3,192,1024]{3,2,1,0:T(8,128)(2,1)S(1)}, bf16[2,3,192,1024]{3,2,1,0:T(8,128)(2,1)}, u32[]{:S(2)}) copy-start(bf16[2,3,192,1024]{3,2,1,0:T(8,128)(2,1)} %copy-done.12) | copy-start | bytes 7077892
  119.1 4.8 %copy-start.15 = (bf16[2,3,192,1024]{3,2,1,0:T(8,128)(2,1)S(1)}, bf16[2,3,192,1024]{3,2,1,0:T(8,128)(2,1)}, u32[]{:S(2)}) copy-start(bf16[2,3,192,1024]{3,2,1,0:T(8,128)(2,1)} %copy-done.14) | copy-start | bytes 7077892
  121.0 2.9 copy-start.29
  125.3 4.6 %copy-start.20 = (bf16[2,3,16,64,64]{4,3,0,2,1:T(8,128)(2,1)S(1)}, bf16[2,3,16,64,64]{4,3,0,2,1:T(8,128)(2,1)}, u32[]{:S(2)}) copy-start(bf16[2,3,16,64,64]{4,3,0,2,1:T(8,128)(2,1)} %copy.199) | copy-start | bytes 2359300
  132.2 25.6 %copy-start.41 = (bf16[2,288,192]{2,1,0:T(8,128)(2,1)S(1)}, bf16[2,288,192]{2,1,0:T(8,128)(2,1)}, u32[]{:S(2)}) copy-start(bf16[2,288,192]{2,1,0:T(8,128)(2,1)} %get-tuple-element.23) | copy-start | bytes 663556
  132.2 25.6 %copy-start.42 = (f32[128,576]{0,1:T(8,128)S(1)}, f32[128,576]{0,1:T(8,128)}, u32[]{:S(2)}) copy-start(f32[128,576]{0,1:T(8,128)} %fusion.50) | copy-start | bytes 884740
  157.6 3.2 copy-start.35
  157.8 2.9 copy-start.48
  165.3 3.6 %copy-start.49 = (bf16[128,192]{0,1:T(8,128)(2,1)S(1)}, bf16[128,192]{0,1:T(8,128)(2,1)}, u32[]{:S(2)}) copy-start(bf16[128,192]{0,1:T(8,128)(2,1)} %copy-done.48) | copy-start | bytes 147460
  165.3 4.7 %copy-start.51 = (bf16[128,192]{0,1:T(8,128)(2,1)S(1)}, bf16[128,192]{0,1:T(8,128)(2,1)}, u32[]{:S(2)}) copy-start(bf16[128,192]{0,1:T(8,128)(2,1)} %copy-done.50) | copy-start | bytes 147460
  167.6 5.1 %copy-start.23 = (f32[128,576]{0,1:T(8,128)S(1)}, f32[128,576]{0,1:T(8,128)}, u32[]{:S(2)}) copy-start(f32[128,576]{0,1:T(8,128)} %copy-done.22) | copy-start | bytes 884740
  167.6 5.1 %copy-start.37 = (bf16[128,576]{0,1:T(8,128)(2,1)S(1)}, bf16[128,576]{0,1:T(8,128)(2,1)}, u32[]{:S(2)}) copy-start(bf16[128,576]{0,1:T(8,128)(2,1)} %reshape.457) | copy-start | bytes 442372
  167.6 6.3 %copy-start.26 = (bf16[128,576]{0,1:T(8,128)(2,1)S(1)}, bf16[128,576]{0,1:T(8,128)(2,1)}, u32[]{:S(2)}) copy-start(bf16[128,576]{0,1:T(8,128)(2,1)} %copy-done.25) | copy-start | bytes 442372
  170.0 6.8 %copy-start.32 = (bf16[128,1536]{1,0:T(8,128)(2,1)S(1)}, bf16[128,1536]{1,0:T(8,128)(2,1)}, u32[]{:S(2)}) copy-start(bf16[128,1536]{1,0:T(8,128)(2,1)} %get-tuple-element.54) | copy-start | bytes 1179652
  173.9 4.7 %copy-start.39 = (bf16[576,192]{1,0:T(8,128)(2,1)S(1)}, bf16[576,192]{1,0:T(8,128)(2,1)}, u32[]{:S(2)}) copy-start(bf16[576,192]{1,0:T(8,128)(2,1)} %copy.207) | copy-start | bytes 663556
  188.2 9.9 %copy-start.56 = (bf16[2,1,16,128]{3,1,2,0:T(2,128)(2,1)S(1)}, bf16[2,1,16,128]{3,1,2,0:T(2,128)(2,1)}, u32[]{:S(2)}) copy-start(bf16[2,1,16,128]{3,1,2,0:T(2,128)(2,1)} %reshape.489) | copy-start | bytes 24580
  (32 other events, 52.4 us)

commit v2 on v1

--- a/solution.py
+++ b/solution.py
@@ -12,14 +12,24 @@
 HEAD_DIM = 64
 LANES = 128
 CHUNKS = 3
-EXTRA_ROWS = 16
 
 epsilon = 1e-05
 theta_base = 100000.0
 masked_value = -1e30
 MESH = pl.DeviceIdType.MESH
 
-ORDERS = ((2, 1, 0), (1, 0, 2), (0, 2, 1))
+ORDERS = ((0, 2, 1), (2, 1, 0), (1, 2, 0), (2, 1, 0), (1, 2, 0), (2, 1, 0))
+PIECES = len(ORDERS)
+
+
+def piece_rows(rows):
+    first = (rows + 31) // 32 * 16
+    return ((0, first), (first, rows - first))
+
+
+def piece_of(ref, piece, rows, lead=3):
+    start, count = piece_rows(rows)[piece % 2]
+    return ref.at[(piece // 2, *[slice(None)] * lead, pl.ds(start, count))]
 
 
 def ctx_dims(count):
@@ -169,13 +179,13 @@
 
 def run_scatter(links, sources, slots, sums, finals, ready=None):
     pending = []
-    for chunk in range(CHUNKS):
+    for chunk in range(PIECES):
         if ready is not None:
             ready(chunk)
         pending.append(scatter_begin(links, ORDERS[chunk], 0, sources[chunk], slots[chunk][0]))
     current = list(sources)
     for stage in range(3):
-        for chunk in range(CHUNKS):
+        for chunk in range(PIECES):
             order = ORDERS[chunk]
             if stage < 2:
                 target = sums[chunk][stage]
@@ -198,14 +208,14 @@
 
 
 def run_gather(links, helds):
-    pending = [None] * CHUNKS
+    pending = [None] * PIECES
     for stage in (2, 1, 0):
-        for chunk in range(CHUNKS):
+        for chunk in range(PIECES):
             if pending[chunk] is not None:
                 for copy in pending[chunk]:
                     copy.wait_recv()
             pending[chunk] = gather_begin(links, ORDERS[chunk], stage, helds[chunk])
-    for chunk in range(CHUNKS):
+    for chunk in range(PIECES):
         for copy in pending[chunk]:
             copy.wait_recv()
 
@@ -269,7 +279,7 @@
     for chunk in range(CHUNKS):
         held[(chunk, *links.coords)] = kv[chunk]
     copies, own = gather_weights_begin(links, fsdp_count, shards, fulls, local_sem)
-    run_gather(links, [held.at[chunk] for chunk in range(CHUNKS)])
+    run_gather(links, [piece_of(held, piece, kv.shape[1]) for piece in range(PIECES)])
     for copy in own:
         copy.wait()
     for copy in copies:
@@ -279,7 +289,7 @@
 
 def gather_kv(kv, shards, fsdp_count, dims, collective_id):
     count = len(shards)
-    total = count * (fsdp_count - 1) + CHUNKS * copies_needed(dims)
+    total = count * (fsdp_count - 1) + PIECES * copies_needed(dims)
     results = pl.pallas_call(
         functools.partial(kv_gather_kernel, count, fsdp_count, dims),
         out_shape=[jax.ShapeDtypeStruct((CHUNKS, *dims, *kv.shape[1:]), kv.dtype)]
@@ -304,39 +314,44 @@
 def kv_scatter_kernel(dims, *refs):
     parts, out = refs[0], refs[1]
     refs = refs[2:]
-    slots = [refs[5 * c : 5 * c + 3] for c in range(CHUNKS)]
-    sums = [refs[5 * c + 3 : 5 * c + 5] for c in range(CHUNKS)]
-    send_sem, recv_sem = refs[5 * CHUNKS :]
+    slots = [refs[5 * c : 5 * c + 3] for c in range(PIECES)]
+    sums = [refs[5 * c + 3 : 5 * c + 5] for c in range(PIECES)]
+    send_sem, recv_sem = refs[5 * PIECES :]
     links = Links(send_sem, recv_sem, dims)
     greet(links, 1)
 
-    def final(chunk):
+    rows = parts.shape[-2]
+
+    def final(piece):
+        target = piece_of(out, piece, rows, 0)
+
         def store(places, value):
-            out[chunk] = value
+            target[...] = value
 
         return store
 
     run_scatter(
         links,
-        [parts.at[chunk] for chunk in range(CHUNKS)],
+        [piece_of(parts, piece, rows) for piece in range(PIECES)],
         slots,
         sums,
-        [final(chunk) for chunk in range(CHUNKS)],
+        [final(piece) for piece in range(PIECES)],
     )
     links.finish()
 
 
 def scatter_scratch(dims, tail):
     scratch = []
-    for order in ORDERS:
-        slots, sums = stage_shapes(dims, order, tail)
+    for piece, order in enumerate(ORDERS):
+        count = piece_rows(tail[0])[piece % 2][1]
+        slots, sums = stage_shapes(dims, order, (count, tail[1]))
         scratch += [pltpu.VMEM(shape, jnp.bfloat16) for shape in slots + sums]
     return scratch
 
 
 def scatter_kv(parts, dims, collective_id):
     tail = parts.shape[-2:]
-    total = CHUNKS * copies_needed(dims)
+    total = PIECES * copies_needed(dims)
     return pl.pallas_call(
         functools.partial(kv_scatter_kernel, dims),
         out_shape=jax.ShapeDtypeStruct((CHUNKS, *tail), jnp.float32),
@@ -355,56 +370,62 @@
     grads, out = refs[0], refs[1]
     arrived, current = refs[2], refs[3]
     refs = refs[4:]
-    slots = [refs[5 * c : 5 * c + 3] for c in range(CHUNKS)]
-    sums = [refs[5 * c + 3 : 5 * c + 5] for c in range(CHUNKS)]
-    send_sem, recv_sem = refs[5 * CHUNKS :]
+    slots = [refs[5 * c : 5 * c + 3] for c in range(PIECES)]
+    sums = [refs[5 * c + 3 : 5 * c + 5] for c in range(PIECES)]
+    send_sem, recv_sem = refs[5 * PIECES :]
     links = Links(send_sem, recv_sem, dims)
     greet(links, fsdp_count)
     mine = lax.axis_index("fsdp")
+    rows = grads.shape[-2]
     first = []
-    for chunk in range(CHUNKS):
+    for piece in range(PIECES):
         first.append([])
         for step in range(1, fsdp_count):
             device = lax.rem(mine + step, fsdp_count)
-            first[chunk].append(
+            first[piece].append(
                 links.send(
-                    grads.at[device, chunk], arrived.at[step - 1, chunk], {"fsdp": device}
+                    piece_of(grads.at[device], piece, rows),
+                    piece_of(arrived.at[step - 1], piece, rows),
+                    {"fsdp": device},
                 )
             )
 
-    def ready(chunk):
-        for copy in first[chunk]:
+    def ready(piece):
+        for copy in first[piece]:
             copy.wait_recv()
+        target = piece_of(current, piece, rows)
 
         def store(places, value):
-            current[(chunk, *places)] = value.astype(current.dtype)
-
-        parts = [lambda places: grads[(mine, chunk, *places)]]
+            target[places] = value.astype(current.dtype)
+
+        views = [piece_of(grads.at[mine], piece, rows)]
         for step in range(fsdp_count - 1):
-            parts.append(lambda places, step=step: arrived[(step, chunk, *places)])
-        add_blocks(store, parts, dims)
-
-    def final(chunk):
+            views.append(piece_of(arrived.at[step], piece, rows))
+        add_blocks(store, [lambda places, view=view: view[places] for view in views], dims)
+
+    def final(piece):
+        target = piece_of(out, piece, rows)
+
         def store(places, value):
-            out[(chunk, *links.coords)] = value.astype(out.dtype)
+            target[links.coords] = value.astype(out.dtype)
 
         return store
 
     run_scatter(
         links,
-        [current.at[chunk] for chunk in range(CHUNKS)],
+        [piece_of(current, piece, rows) for piece in range(PIECES)],
         slots,
         sums,
-        [final(chunk) for chunk in range(CHUNKS)],
+        [final(piece) for piece in range(PIECES)],
         ready,
     )
-    run_gather(links, [out.at[chunk] for chunk in range(CHUNKS)])
+    run_gather(links, [piece_of(out, piece, rows) for piece in range(PIECES)])
     links.finish()
 
 
 def sum_grads(grads, fsdp_count, dims, collective_id):
     tail = grads.shape[-2:]
-    total = CHUNKS * (2 * copies_needed(dims) + fsdp_count - 1)
+    total = PIECES * (2 * copies_needed(dims) + fsdp_count - 1)
     return pl.pallas_call(
         functools.partial(sum_grads_kernel, fsdp_count, dims),
         out_shape=jax.ShapeDtypeStruct((CHUNKS, *dims, *tail), grads.dtype),
@@ -421,6 +442,49 @@
         ),
         name="sum_grads",
     )(grads)
+
+
+def pack_kernel(ff_shard, normed, attended, normed_two, top, qkv, branch, gate, up, inner, gains, out):
+    fsdp_count, shard_rows, _ = normed.shape
+    extra = out.shape[2] - shard_rows
+
+    def product(left, right):
+        return jnp.dot(left, right, preferred_element_type=jnp.float32)
+
+    def body(owner, carry):
+        def put(tile, value):
+            out[owner, tile, :shard_rows, :] = value.astype(out.dtype)
+            if tile:
+                out[owner, tile, shard_rows:, :] = jnp.zeros((extra, LANES), out.dtype)
+
+        def column(ref, place):
+            return ref[:, place * LANES : (place + 1) * LANES]
+
+        out[owner, 0, shard_rows:, :] = gains[owner]
+        one, two, three = normed[owner], attended[owner], normed_two[owner]
+        tile = 0
+        last = qkv.shape[1] // LANES - 1
+        for place in range(last):
+            put(tile, product(one, column(qkv, place)))
+            tile += 1
+        put(tile, product(one, column(qkv, last)) + product(two, column(branch, 0)))
+        tile += 1
+        for place in range(1, branch.shape[1] // LANES):
+            put(tile, product(two, column(branch, place)))
+            tile += 1
+        for ref in (gate, up):
+            for place in range(ref.shape[1] // LANES):
+                put(tile, product(three, column(ref, place)))
+                tile += 1
+        for place in range(ff_shard // LANES):
+            start = pl.multiple_of(owner * ff_shard + place * LANES, LANES)
+            right = inner[:, pl.ds(start, LANES)]
+            for part in range(fsdp_count):
+                put(tile, product(top[part], right))
+                tile += 1
+        return carry
+
+    lax.fori_loop(0, fsdp_count, body, 0)
 
 
 def make_tables(positions):
@@ -584,14 +648,11 @@
     y_out = result.reshape(seq_count, tok_count, model_width).astype(jnp.bfloat16)
     grad_top = out_grad.reshape(rows_all, model_width)
     grad_residual = grad_top.astype(jnp.float32)
-    grad_wdown = jnp.einsum("rf,rd->fd", inner_rows, grad_top, preferred_element_type=jnp.float32)
     grad_inner = jnp.einsum("rd,fd->rf", grad_top, full_down, preferred_element_type=jnp.float32)
     grad_gate = (
         grad_inner * up_vals * sigmoid_gate * (1.0 + gate_vals * (1.0 - sigmoid_gate))
     ).astype(jnp.bfloat16)
     grad_up = (grad_inner * activated).astype(jnp.bfloat16)
-    grad_wgate = jnp.einsum("rd,rf->df", normed_two, grad_gate, preferred_element_type=jnp.float32)
-    grad_wup = jnp.einsum("rd,rf->df", normed_two, grad_up, preferred_element_type=jnp.float32)
     grad_normed_two = jnp.einsum(
         "rf,df->rd", grad_gate, full_gate, preferred_element_type=jnp.float32
     ) + jnp.einsum("rf,df->rd", grad_up, full_up, preferred_element_type=jnp.float32)
@@ -600,7 +661,6 @@
     )
     grad_hidden = grad_residual + grad_hidden_norm
     grad_branch = grad_hidden.astype(jnp.bfloat16)
-    grad_wout = jnp.einsum("ri,rj->ij", attended, grad_branch, preferred_element_type=jnp.float32)
     grad_attended = jnp.einsum(
         "rj,ij->ri", grad_branch, full_out, preferred_element_type=jnp.float32
     ).astype(jnp.bfloat16)
@@ -654,13 +714,6 @@
         .reshape(rows_all, KV_HEADS * HEAD_DIM)
     )
     grad_value_low = grad_value.astype(jnp.bfloat16).reshape(rows_all, KV_HEADS * HEAD_DIM)
-    grad_wquery = jnp.einsum(
-        "rd,re->de", normed, grad_query_low, preferred_element_type=jnp.float32
-    )
-    grad_wkey = jnp.einsum("rd,re->de", normed, grad_key_low, preferred_element_type=jnp.float32)
-    grad_wvalue = jnp.einsum(
-        "rd,re->de", normed, grad_value_low, preferred_element_type=jnp.float32
-    )
     grad_normed = jnp.einsum(
         "re,de->rd", grad_query_low, full_query, preferred_element_type=jnp.float32
     )
@@ -679,23 +732,14 @@
         .reshape(seq_count, tok_count, model_width)
     )
     shard_rows = model_width // fsdp_count
-    wide = [grad_wquery, grad_wkey, grad_wvalue, grad_wout, grad_wgate, grad_wup]
-    widths = [grad.shape[1] for grad in wide]
-    columns = jnp.concatenate([grad.astype(jnp.bfloat16) for grad in wide], axis=1)
-    wide_tiles = columns.shape[1] // LANES
-    columns = columns.reshape(fsdp_count, shard_rows, wide_tiles, LANES).transpose(0, 2, 1, 3)
-    hidden = grad_wdown.shape[0]
+    extra_rows = 16 + -shard_rows % 16
+    hidden = inner_rows.shape[1]
+    ff_shard = hidden // fsdp_count
+    aligned = ff_shard % LANES == 0
+    widths = [model_width, KV_HEADS * HEAD_DIM, KV_HEADS * HEAD_DIM, model_width, hidden, hidden]
+    wide_tiles = sum(widths) // LANES
     half_hidden = hidden // (2 * fsdp_count)
     down_tiles = 2 * model_width // LANES
-    down = (
-        grad_wdown.astype(jnp.bfloat16)
-        .reshape(fsdp_count, 2, half_hidden, model_width)
-        .transpose(0, 2, 1, 3)
-        .reshape(fsdp_count, half_hidden, down_tiles, LANES)
-        .transpose(0, 2, 1, 3)
-        .reshape(fsdp_count, -1, shard_rows, LANES)
-    )
-    tiles = jnp.concatenate([columns, down], axis=1)
     gains = (
         jnp.stack([grad_gain_attn, grad_gain_mlp])
         .astype(jnp.bfloat16)
@@ -703,19 +747,72 @@
         .transpose(1, 0, 2)
         .reshape(fsdp_count, 2 * shard_rows)
     )
-    used_tiles = tiles.shape[1]
+    gains = jnp.pad(gains, ((0, 0), (0, extra_rows * LANES - 2 * shard_rows))).reshape(
+        fsdp_count, extra_rows, LANES
+    )
+    if aligned:
+        used_tiles = wide_tiles + ff_shard // LANES * fsdp_count
+
+        def turned(rows):
+            return rows.T.reshape(fsdp_count, shard_rows, rows_all)
+
+        blank = jnp.zeros((rows_all, LANES // 2), jnp.bfloat16)
+        packed = pl.pallas_call(
+            functools.partial(pack_kernel, ff_shard),
+            out_shape=jax.ShapeDtypeStruct(
+                (fsdp_count, used_tiles, shard_rows + extra_rows, LANES), jnp.bfloat16
+            ),
+            compiler_params=pltpu.CompilerParams(vmem_limit_bytes=32 << 20),
+            name="pack_grads",
+        )(
+            turned(normed),
+            turned(attended),
+            turned(normed_two),
+            turned(grad_top),
+            jnp.concatenate([grad_query_low, grad_key_low, grad_value_low, blank], axis=1),
+            jnp.concatenate([blank, grad_branch], axis=1),
+            grad_gate,
+            grad_up,
+            inner_rows,
+            gains,
+        )
+    else:
+
+        def summed_rows(left, right):
+            return jnp.einsum("ri,rj->ij", left, right, preferred_element_type=jnp.float32).astype(
+                jnp.bfloat16
+            )
+
+        columns = jnp.concatenate(
+            [
+                summed_rows(normed, grad_query_low),
+                summed_rows(normed, grad_key_low),
+                summed_rows(normed, grad_value_low),
+                summed_rows(attended, grad_branch),
+                summed_rows(normed_two, grad_gate),
+                summed_rows(normed_two, grad_up),
+            ],
+            axis=1,
+        )
+        columns = columns.reshape(fsdp_count, shard_rows, wide_tiles, LANES).transpose(0, 2, 1, 3)
+        down = (
+            summed_rows(inner_rows, grad_top)
+            .reshape(fsdp_count, 2, half_hidden, model_width)
+            .transpose(0, 2, 1, 3)
+            .reshape(fsdp_count, half_hidden, down_tiles, LANES)
+            .transpose(0, 2, 1, 3)
+            .reshape(fsdp_count, -1, shard_rows, LANES)
+        )
+        tiles = jnp.concatenate([columns, down], axis=1)
+        used_tiles = tiles.shape[1]
+        gains = jnp.pad(gains[:, None], ((0, 0), (0, used_tiles - 1), (0, 0), (0, 0)))
+        packed = jnp.concatenate([tiles, gains], axis=2)
     tile_count = used_tiles + -used_tiles % (CHUNKS * ctx_count)
-    tiles = jnp.pad(tiles, ((0, 0), (0, tile_count - used_tiles), (0, 0), (0, 0)))
-    gains = jnp.pad(gains, ((0, 0), (0, EXTRA_ROWS * LANES - 2 * shard_rows)))
-    gains = jnp.pad(
-        gains.reshape(fsdp_count, 1, EXTRA_ROWS, LANES),
-        ((0, 0), (0, tile_count - 1), (0, 0), (0, 0)),
-    )
-    packed = jnp.concatenate([tiles, gains], axis=2).reshape(
-        fsdp_count, CHUNKS, *dims, shard_rows + EXTRA_ROWS, LANES
-    )
+    if tile_count != used_tiles:
+        packed = jnp.pad(packed, ((0, 0), (0, tile_count - used_tiles), (0, 0), (0, 0)))
+    packed = packed.reshape(fsdp_count, CHUNKS, *dims, shard_rows + extra_rows, LANES)
     summed = sum_grads(packed, fsdp_count, dims, 3).reshape(
-        tile_count, shard_rows + EXTRA_ROWS, LANES
+        tile_count, shard_rows + extra_rows, LANES
     )
     gains = summed[0, shard_rows:].astype(jnp.float32).reshape(-1)
     columns = (
@@ -728,15 +825,17 @@
     for width in widths:
         owned.append(columns[:, offset : offset + width])
         offset += width
-    down = (
-        summed[wide_tiles:used_tiles, :shard_rows]
-        .reshape(down_tiles, half_hidden, LANES)
-        .transpose(1, 0, 2)
-        .reshape(half_hidden, 2, model_width)
-        .transpose(1, 0, 2)
-        .reshape(2 * half_hidden, model_width)
-        .astype(jnp.float32)
-    )
+    down = summed[wide_tiles:used_tiles, :shard_rows]
+    if aligned:
+        down = down.reshape(-1, fsdp_count, shard_rows, LANES).transpose(0, 3, 1, 2)
+    else:
+        down = (
+            down.reshape(down_tiles, half_hidden, LANES)
+            .transpose(1, 0, 2)
+            .reshape(half_hidden, 2, model_width)
+            .transpose(1, 0, 2)
+        )
+    down = down.reshape(ff_shard, model_width).astype(jnp.float32)
     return (
         y_out,
         x_grad,

time: 331 us -> 259 us (0.78)
  local copies, waits for them, and re-layouts: 87.5 us -> 52.7 us
  Pallas kernels: 182 us -> 158 us
  matrix products: 35.1 us -> 26.8 us
  other arithmetic: 23.3 us -> 17.8 us
    reshape x7 -> x0, local copies, waits for them, and re-layouts: 17 us -> none  [the longest x1 9.91 us: local(): columns.reshape(fsdp_count, shard_rows, wide_tiles, LANES)]
    pallas_call x1, Pallas kernels: 111 us -> 94.6 us  [sum_grads(): pl.pallas_call(functools.partial(sum_grads_kernel, fsdp_count, dims), out...]
    concatenate x4 -> x2, local copies, waits for them, and re-layouts: 15.5 us -> 0.19 us  [the longest x1 0.11 us: local(): jnp.concatenate([blank, grad_branch], axis=1)]
    dot_general x7 -> x0, matrix products: 9.82 us -> none  [the longest x1 2.86 us: local(): jnp.einsum('rd,rf->df', normed_two, grad_gate, preferred_element_type=jnp...]
    convert_element_type x6 -> x1, local copies, waits for them, and re-layouts: 7.95 us -> 1.07 us  [local(): down = down.reshape(ff_shard, model_width).astype(jnp.float32)]
    pallas_call x1, Pallas kernels: 24.9 us -> 18.2 us  [scatter_kv(): pl.pallas_call(functools.partial(kv_scatter_kernel, dims), out_shape=jax....]
    concatenate x3 -> x1, other arithmetic: 6.42 us -> 0.1 us  [local(): jnp.concatenate([grad_query_low, grad_key_low, grad_value_low, blank], ax...]
    unnamed x132 -> x125, local copies, waits for them, and re-layouts: 13.9 us -> 17.1 us
where the time goes in v2:
time: 259 us; the launch traced here: 257 us
  Pallas kernels  158 us (61%)
  local copies, waits for them, and re-layouts  52.7 us (20%)
  matrix products  26.8 us (10%)
  other arithmetic  17.8 us (7%)
    pallas_call x1, Pallas kernels, sum_grads(): pl.pallas_call(functools.partial(sum_grads_kernel, fsdp_count, dims), out...  94.6 us
    pallas_call x1, Pallas kernels, gather_weights(): pl.pallas_call(functools.partial(weights_kernel, count, fsdp_count, dims)...  22 us
    pallas_call x1, Pallas kernels, gather_kv(): pl.pallas_call(functools.partial(kv_gather_kernel, count, fsdp_count, dim...  21.2 us
    pallas_call x1, Pallas kernels, scatter_kv(): pl.pallas_call(functools.partial(kv_scatter_kernel, dims), out_shape=jax....  18.2 us
    unnamed x125, local copies, waits for them, and re-layouts  17.1 us
    concatenate x4, local copies, waits for them, and re-layouts, local(): jnp.concatenate([grad_key_part, grad_value_part], axis=-1)  9.31 us
    sub x1, other arithmetic, local(): weights = jnp.where(visible, jnp.exp(scores - top), 0.0)  6.12 us

profile of v2, /device:TPU:27, one launch (start us, length us, event | category | flops | bytes accessed | tf_op | source)
XLA Modules:
  0.0 257.1 jit_solution(1071390680606295737)
XLA Ops:
  1.9 22.0 %gather_weights.1 = (bf16[2,288,576]{2,1,0:T(8,128)(2,1)}, bf16[2,288,192]{2,1,0:T(8,128)(2,1)}, bf16[2,288,192]{2,1,0:T(8,128)(2,1)}, bf16[2,1,288]{2,1,0:T(2,128)(2,1)}) custom-call(bf16[288,576]{1,0:T(8,128)(2,1)} %refs_0_.1, bf16[288,192]{1,0:T(8,128)(2,1)} %refs_1_.2, bf16[288,192]{1,0:T(8,128)(2,1)} %refs_2_.2, bf16[1,288]{1,0:T(2,128)(2,1)} %reshape.406.refs_3_), custom_call_target="tpu_custom_call" | custom-call | tf_op jit(solution)/shard_map/gather_weights/pallas_call | solution.py:257
  24.0 1.5 copy.182
  39.4 21.2 %gather_kv.1 = (bf16[3,4,2,2,128,128]{5,4,3,2,1,0:T(8,128)(2,1)S(1)}, bf16[2,288,576]{2,1,0:T(8,128)(2,1)S(1)}, bf16[2,288,1536]{2,1,0:T(8,128)(2,1)S(1)}, bf16[...) custom-call(bf16[3,128,128]{2,1,0:T(8,128)(2,1)S(1)} %copy-done.14, ...), custom_call_target="tpu_custom_call" | custom-call | tf_op jit(solution)/shard_map/gather_kv/pallas_call | solution.py:293
  61.8 2.9 %fusion.9 = f32[2,3,192,1024]{3,2,1,0:T(8,128)} fusion(bf16[2,3,192,64]{3,2,1,0:T(8,128)(2,1)S(1)} %bitcast.199, bf16[2,3,1024,128]{3,2,1,0:T(8,128)(2,1)S(1)} %bitcast.189), kind=kOutput, calls=%fused_computation.21 | convolution fusion | flops 150994944 | bytes 6438912 | tf_op jit(solution)/shard_map/skqd,sknd->skqn/dot_general | solution.py:622
  66.4 6.1 %fusion.42 = (f32[2,3,192]{2,1,0:T(4,128)S(1)}, f32[2,3,192,1024]{3,2,1,0:T(8,128)S(1)}) fusion(f32[2,3,192,1024]{3,2,1,0:T(8,128)} %fusion.9, pred[192,1024]{1,0:T(8,128)(4,1)S(1)} %broadcast_compare_fusion), kind=kOutput, calls=%fused_computation.117 | output fusion | flops 8258559 | bytes 9638400 | tf_op jit(solution)/shard_map/sub | solution.py:627
  73.1 1.5 copy-done.27
  75.1 2.3 fusion.43
  77.4 1.8 copy.194
  79.2 1.9 copy.195
  81.1 1.8 reshape.415
  82.9 2.3 multiply_reduce_fusion.5
  85.3 1.6 fusion.44
  87.5 1.7 multiply_convert_fusion.2
  91.0 1.8 fusion.46
  95.3 3.2 %multiply_convert_fusion = bf16[2,3,192,1024]{3,2,1,0:T(8,128)(2,1)S(1)} fusion(f32[2,3,192]{2,1,0:T(4,128)S(1)} %multiply_reduce_fusion, bf16[2,3,192,64]{3,2,1,0:T(8,128)(2,1)S(1)} %bitcast.202, f32[2,3,192,1024]{3,2,1,0:T(8,128)} %copy-done.27, f32[2,3,192]{2,1,0:T(4,128)S(1)} %copy-done.52, bf16[2,3,1024,128]{3,2,1,0:T(8,128)(2,1)S(1)} %bitcast.191), kind=kOutput, calls=%fused_computation.3 | convolution fusion | flops 155713536 | bytes 8807424 | tf_op jit(solution)/shard_map/skqd,sknd->skqn/dot_general | solution.py:676
  98.6 1.4 copy-done.24
  101.9 2.2 copy.205
  106.4 1.8 convert_element_type.175
  108.2 2.0 fusion.47
  110.2 1.5 convolution_convert_fusion
  111.8 1.9 concatenate.55
  113.7 2.8 %copy.210 = bf16[2,3,16,64,64]{4,3,0,2,1:T(8,128)(2,1)} copy(bf16[2,3,16,64,64]{3,2,4,1,0:T(8,128)(2,1)} %concatenate.55) | data formatting | bytes 1572864 | tf_op jit(solution)/shard_map/concatenate | solution.py:688
  116.5 1.5 multiply_convert_fusion.1
  118.0 2.6 %concatenate.54 = bf16[2,3,16,64,64]{3,2,4,1,0:T(8,128)(2,1)S(1)} reshape(bf16[2,3,1024,64]{2,3,1,0:T(8,128)(2,1)} %multiply_convert_fusion.1) | data formatting | bytes 1572864 | tf_op jit(solution)/shard_map/concatenate | solution.py:688
  120.6 2.0 copy.209
  122.6 2.3 pad_maximum_fusion
  124.9 18.2 %scatter_kv.1 = f32[3,128,128]{2,1,0:T(8,128)S(1)} custom-call(bf16[3,4,2,2,128,128]{5,4,3,2,1,0:T(8,128)(2,1)S(1)} %bitcast.176), custom_call_target="tpu_custom_call" | custom-call | tf_op jit(solution)/shard_map/scatter_kv/pallas_call | solution.py:355
  148.9 2.2 pack_grads.1
  151.1 2.9 %copy-done = bf16[2,48,304,128]{3,2,1,0:T(8,128)(2,1)} copy-done((bf16[2,48,304,128]{3,2,1,0:T(8,128)(2,1)}, bf16[2,48,304,128]{3,2,1,0:T(8,128)(2,1)S(1)}, u32[]{:S(2)}) %copy-start) | copy-done | bytes 7471128
  154.0 94.6 %sum_grads.1 = bf16[3,4,2,2,304,128]{5,4,3,2,1,0:T(8,128)(2,1)S(1)} custom-call(bf16[2,3,4,2,2,304,128]{6,5,4,3,2,1,0:T(8,128)(2,1)} %bitcast.168), custom_call_target="tpu_custom_call" | custom-call | tf_op jit(solution)/shard_map/sum_grads/pallas_call | solution.py:429
  252.2 2.0 fusion.37
  255.5 1.6 copy.254
  (209 shorter events, 38.1 us)
Async XLA Ops:
  0.6 27.3 %copy-start.28 = (bf16[2,64,576]{2,1,0:T(8,128)(2,1)S(1)}, bf16[2,64,576]{2,1,0:T(8,128)(2,1)}, u32[]{:S(2)}) copy-start(bf16[2,64,576]{2,1,0:T(8,128)(2,1)} %param.12) | copy-start | bytes 442372
  0.7 27.8 %copy-start.58 = (s32[32]{0:T(128)S(1)}, s32[32]{0:T(128)}, u32[]{:S(2)}) copy-start(s32[32]{0:T(128)} %param.22) | copy-start | bytes 388
  26.2 4.4 %copy-start.42 = (bf16[2,288,192]{2,1,0:T(8,128)(2,1)S(1)}, bf16[2,288,192]{2,1,0:T(8,128)(2,1)}, u32[]{:S(2)}) copy-start(bf16[2,288,192]{2,1,0:T(8,128)(2,1)} %get-tuple-element.24) | copy-start | bytes 663556
  28.0 3.1 %copy-start.44 = (bf16[2,288,192]{2,1,0:T(8,128)(2,1)S(1)}, bf16[2,288,192]{2,1,0:T(8,128)(2,1)}, u32[]{:S(2)}) copy-start(bf16[2,288,192]{2,1,0:T(8,128)(2,1)} %get-tuple-element.23) | copy-start | bytes 663556
  29.2 2.4 copy-start.47
  29.2 2.4 copy-start.49
  29.4 3.3 %copy-start.46 = (bf16[768,576]{0,1:T(8,128)(2,1)S(1)}, bf16[768,576]{0,1:T(8,128)(2,1)}, u32[]{:S(2)}) copy-start(bf16[768,576]{0,1:T(8,128)(2,1)} %param.20) | copy-start | bytes 2654212
  30.7 3.3 %copy-start.57 = (bf16[288]{0:T(512)(128)(2,1)S(1)}, bf16[288]{0:T(512)(128)(2,1)}, u32[]{:S(2)}) copy-start(bf16[288]{0:T(512)(128)(2,1)} %param.21) | copy-start | bytes 1732
  60.6 4.2 %copy-start.2 = (bf16[2,288,576]{2,1,0:T(8,128)(2,1)}, bf16[2,288,576]{2,1,0:T(8,128)(2,1)S(1)}, u32[]{:S(2)}) copy-start(bf16[2,288,576]{2,1,0:T(8,128)(2,1)S(1)} %get-tuple-element.26) | copy-start | bytes 1990660
  60.6 4.1 %copy-start.4 = (bf16[2,768,576]{2,1,0:T(8,128)(2,1)}, bf16[2,768,576]{2,1,0:T(8,128)(2,1)S(1)}, u32[]{:S(2)}) copy-start(bf16[2,768,576]{2,1,0:T(8,128)(2,1)S(1)} %get-tuple-element.30) | copy-start | bytes 5308420
  60.7 4.0 %copy-start.16 = (bf16[3,16,2,64,128]{4,3,1,0,2:T(8,128)(2,1)}, bf16[3,16,2,64,128]{4,3,1,0,2:T(8,128)(2,1)S(1)}, u32[]{:S(2)}) copy-start(bf16[3,16,2,64,128]{4,3,1,0,2:T(8,128)(2,1)S(1)} %copy.190) | copy-start | bytes 4718596
  61.8 3.0 %copy-start.56 = (s32[64]{0:T(128)S(1)}, s32[64]{0:T(128)}, u32[]{:S(2)}) copy-start(s32[64]{0:T(128)} %get-tuple-element.36) | copy-start | bytes 772
  72.5 2.6 %copy-start.17 = (bf16[3,16,2,64,128]{4,3,1,0,2:T(8,128)(2,1)S(1)}, bf16[3,16,2,64,128]{4,3,1,0,2:T(8,128)(2,1)}, u32[]{:S(2)}) copy-start(bf16[3,16,2,64,128]{4,3,1,0,2:T(8,128)(2,1)} %copy-done.16) | copy-start | bytes 4718596
  75.1 2.3 copy-start.19
  91.0 2.7 %copy-start.36 = (bf16[2,64,576]{2,1,0:T(8,128)(2,1)S(1)}, bf16[2,64,576]{2,1,0:T(8,128)(2,1)}, u32[]{:S(2)}) copy-start(bf16[2,64,576]{2,1,0:T(8,128)(2,1)} %param.23) | copy-start | bytes 442372
  94.9 3.6 %copy-start.33 = (bf16[2,64,9,64]{3,1,2,0:T(8,128)(2,1)}, bf16[2,64,9,64]{3,1,2,0:T(8,128)(2,1)S(1)}, u32[]{:S(2)}) copy-start(bf16[2,64,9,64]{3,1,2,0:T(8,128)(2,1)S(1)} %copy.201) | copy-start | bytes 442372
  100.0 4.2 %copy-start.48 = (f32[64,32]{0,1:T(8,128)S(1)}, f32[64,32]{0,1:T(8,128)}, u32[]{:S(2)}) copy-start(f32[64,32]{0,1:T(8,128)} %copy-done.47) | copy-start | bytes 24580
  100.0 4.2 %copy-start.50 = (f32[64,32]{0,1:T(8,128)S(1)}, f32[64,32]{0,1:T(8,128)}, u32[]{:S(2)}) copy-start(f32[64,32]{0,1:T(8,128)} %copy-done.49) | copy-start | bytes 24580
  100.8 7.4 %copy-start.30 = (bf16[2,288,576]{2,1,0:T(8,128)(2,1)S(1)}, bf16[2,288,576]{2,1,0:T(8,128)(2,1)}, u32[]{:S(2)}) copy-start(bf16[2,288,576]{2,1,0:T(8,128)(2,1)} %get-tuple-element.22) | copy-start | bytes 1990660
  101.9 8.4 %copy-start.20 = (bf16[2,3,192,1024]{3,2,1,0:T(8,128)(2,1)S(1)}, bf16[2,3,192,1024]{3,2,1,0:T(8,128)(2,1)}, u32[]{:S(2)}) copy-start(bf16[2,3,192,1024]{3,2,1,0:T(8,128)(2,1)} %copy-done.19) | copy-start | bytes 7077892
  111.8 4.8 %copy-start.25 = (bf16[2,3,192,1024]{3,2,1,0:T(8,128)(2,1)S(1)}, bf16[2,3,192,1024]{3,2,1,0:T(8,128)(2,1)}, u32[]{:S(2)}) copy-start(bf16[2,3,192,1024]{3,2,1,0:T(8,128)(2,1)} %copy-done.24) | copy-start | bytes 7077892
  113.7 2.9 %copy-start.32 = (bf16[2,64,3,3,64]{4,1,3,2,0:T(8,128)(2,1)S(1)}, bf16[2,64,3,3,64]{4,1,3,2,0:T(8,128)(2,1)}, u32[]{:S(2)}) copy-start(bf16[2,64,3,3,64]{4,1,3,2,0:T(8,128)(2,1)} %pad_maximum_fusion.1) | copy-start | bytes 442372
  118.0 4.6 %copy-start.26 = (bf16[2,3,16,64,64]{4,3,0,2,1:T(8,128)(2,1)S(1)}, bf16[2,3,16,64,64]{4,3,0,2,1:T(8,128)(2,1)}, u32[]{:S(2)}) copy-start(bf16[2,3,16,64,64]{4,3,0,2,1:T(8,128)(2,1)} %copy.210) | copy-start | bytes 2359300
  124.9 18.9 %copy-start.41 = (f32[128,576]{1,0:T(8,128)S(1)}, f32[128,576]{1,0:T(8,128)}, u32[]{:S(2)}) copy-start(f32[128,576]{1,0:T(8,128)} %fusion.47) | copy-start | bytes 884740
  124.9 18.9 %copy-start.45 = (bf16[2,288,192]{2,1,0:T(8,128)(2,1)S(1)}, bf16[2,288,192]{2,1,0:T(8,128)(2,1)}, u32[]{:S(2)}) copy-start(bf16[2,288,192]{2,1,0:T(8,128)(2,1)} %get-tuple-element.23) | copy-start | bytes 663556
  144.3 3.7 %copy-start.40 = (bf16[128,576]{0,1:T(8,128)(2,1)S(1)}, bf16[128,576]{0,1:T(8,128)(2,1)}, u32[]{:S(2)}) copy-start(bf16[128,576]{0,1:T(8,128)(2,1)} %convert_element_type.175) | copy-start | bytes 442372
  144.4 4.0 %copy-start.39 = (bf16[128,576]{1,0:T(8,128)(2,1)S(1)}, bf16[128,576]{1,0:T(8,128)(2,1)}, u32[]{:S(2)}) copy-start(bf16[128,576]{1,0:T(8,128)(2,1)} %copy-done.38) | copy-start | bytes 442372
  145.4 3.5 %copy-start.7 = (bf16[128,1536]{1,0:T(8,128)(2,1)S(1)}, bf16[128,1536]{1,0:T(8,128)(2,1)}, u32[]{:S(2)}) copy-start(bf16[128,1536]{1,0:T(8,128)(2,1)} %get-tuple-element.43.up) | copy-start | bytes 1179652
  145.4 3.5 %copy-start.8 = (bf16[128,1536]{1,0:T(8,128)(2,1)S(1)}, bf16[128,1536]{1,0:T(8,128)(2,1)}, u32[]{:S(2)}) copy-start(bf16[128,1536]{1,0:T(8,128)(2,1)} %get-tuple-element.44.gate) | copy-start | bytes 1179652
  145.4 3.5 %copy-start.10 = (bf16[128,1536]{1,0:T(8,128)(2,1)S(1)}, bf16[128,1536]{1,0:T(8,128)(2,1)}, u32[]{:S(2)}) copy-start(bf16[128,1536]{1,0:T(8,128)(2,1)} %copy-done.9) | copy-start | bytes 1179652
  145.4 3.5 %copy-start.11 = (bf16[128,576]{0,1:T(8,128)(2,1)S(1)}, bf16[128,576]{0,1:T(8,128)(2,1)}, u32[]{:S(2)}) copy-start(bf16[128,576]{0,1:T(8,128)(2,1)} %reshape.415) | copy-start | bytes 442372
  151.1 2.9 %copy-start = (bf16[2,48,304,128]{3,2,1,0:T(8,128)(2,1)}, bf16[2,48,304,128]{3,2,1,0:T(8,128)(2,1)S(1)}, u32[]{:S(2)}) copy-start(bf16[2,48,304,128]{3,2,1,0:T(8,128)(2,1)S(1)} %pack_grads.1) | copy-start | bytes 22413316
  (27 other events, 39.7 us)

commit v3 on v2

--- a/solution.py
+++ b/solution.py
@@ -487,6 +487,53 @@
     lax.fori_loop(0, fsdp_count, body, 0)
 
 
+def dot_over(left, right, left_dim, right_dim):
+    return lax.dot_general(
+        left, right, (((left_dim,), (right_dim,)), ((), ())), preferred_element_type=jnp.float32
+    )
+
+
+def keys_values(kv, head, seq):
+    block = kv[head, :, seq]
+    block = block.reshape(block.shape[0] * block.shape[1], block.shape[2])
+    return block[:, :HEAD_DIM], block[:, HEAD_DIM:]
+
+
+def attention_kernel(queries, kv, query_pos, key_pos, out, log_total):
+    visible = query_pos[...] >= key_pos[...]
+    for seq in range(queries.shape[0]):
+        for head in range(KV_HEADS):
+            keys, values = keys_values(kv, head, seq)
+            scores = dot_over(queries[seq, head], keys, 1, 1) * HEAD_DIM ** (-0.5)
+            scores = jnp.where(visible, scores, masked_value)
+            top = jnp.max(scores, axis=-1, keepdims=True)
+            weights = jnp.where(visible, jnp.exp(scores - top), 0.0)
+            total = jnp.sum(weights, axis=-1, keepdims=True)
+            weights = (weights / total).astype(jnp.bfloat16)
+            out[seq, head] = jnp.dot(weights, values, preferred_element_type=jnp.float32)
+            log_total[seq, head] = top + jnp.log(total)
+
+
+def attention_grad_kernel(
+    queries, kv, query_pos, key_pos, grads, delta, log_total, grad_query, grad_kv
+):
+    scale = HEAD_DIM ** (-0.5)
+    visible = query_pos[...] >= key_pos[...]
+    for seq in range(queries.shape[0]):
+        for head in range(KV_HEADS):
+            keys, values = keys_values(kv, head, seq)
+            query, grad = queries[seq, head], grads[seq, head]
+            scores = dot_over(query, keys, 1, 1) * scale
+            weights = jnp.where(visible, jnp.exp(scores - log_total[seq, head]), 0.0)
+            grad_value = dot_over(weights.astype(jnp.bfloat16), grad, 0, 0)
+            grad_weights = dot_over(grad, values, 1, 1)
+            grad_scores = (weights * (grad_weights - delta[seq, head])).astype(jnp.bfloat16)
+            grad_query[seq, head] = jnp.dot(grad_scores, keys, preferred_element_type=jnp.float32)
+            grad_key = dot_over(grad_scores, query, 0, 0) * scale
+            both = jnp.concatenate([grad_key, grad_value], axis=1).astype(jnp.bfloat16)
+            grad_kv[head, :, seq] = both.reshape(kv.shape[1], kv.shape[3], kv.shape[4])
+
+
 def make_tables(positions):
     half_dim = HEAD_DIM // 2
     frequency = theta_base ** (-2.0 * jnp.arange(half_dim, dtype=jnp.float32) / HEAD_DIM)
@@ -606,30 +653,24 @@
         kv_rows, [w_out, w_gate, w_up, w_down, mlp_gain.reshape(1, -1)], fsdp_count, dims, 1
     )
     gain_mlp_f = gain_mlp.reshape(-1).astype(jnp.float32)
-    kv_all = (
-        kv_all.reshape(KV_HEADS, ctx_count, seq_count, tok_count, 2 * HEAD_DIM)
-        .transpose(2, 0, 1, 3, 4)
-        .reshape(seq_count, KV_HEADS, ctx_count * tok_count, 2 * HEAD_DIM)
-    )
-    key_all = kv_all[..., :HEAD_DIM]
-    value_all = kv_all[..., HEAD_DIM:]
+    kv_all = kv_all.reshape(KV_HEADS, ctx_count, seq_count, tok_count, 2 * HEAD_DIM)
     queries = queries.transpose(0, 2, 3, 1, 4).reshape(
         seq_count, KV_HEADS, group_size * tok_count, HEAD_DIM
     )
     key_pos = slot_positions(block_of_slot, jnp.int32(0), ctx_count * tok_count, half_len)
-    visible = jnp.tile(query_pos, group_size)[:, None] >= key_pos[None, :]
-    scores = (
-        jnp.einsum("skqd,sknd->skqn", queries, key_all, preferred_element_type=jnp.float32)
-        * score_scale
-    )
-    scores = jnp.where(visible, scores, masked_value)
-    top = jnp.max(scores, axis=-1, keepdims=True)
-    weights = jnp.where(visible, jnp.exp(scores - top), 0.0)
-    weights = weights / jnp.sum(weights, axis=-1, keepdims=True)
-    weights_low = weights.astype(jnp.bfloat16)
-    attended_f = jnp.einsum(
-        "skqn,sknd->skqd", weights_low, value_all, preferred_element_type=jnp.float32
-    )
+    row_pos = jnp.tile(query_pos, group_size)[:, None]
+    key_pos = key_pos[None, :]
+    local_params = pltpu.CompilerParams(vmem_limit_bytes=40 << 20)
+    head_shape = queries.shape
+    attended_f, log_total = pl.pallas_call(
+        attention_kernel,
+        out_shape=[
+            jax.ShapeDtypeStruct(head_shape, jnp.float32),
+            jax.ShapeDtypeStruct((*head_shape[:-1], 1), jnp.float32),
+        ],
+        compiler_params=local_params,
+        name="attention",
+    )(queries, kv_all, row_pos, key_pos)
     attended = (
         attended_f.astype(jnp.bfloat16)
         .reshape(seq_count, HEADS, tok_count, HEAD_DIM)
@@ -670,27 +711,16 @@
         .reshape(seq_count, KV_HEADS, group_size * tok_count, HEAD_DIM)
     )
     row_delta = jnp.sum(grad_heads.astype(jnp.float32) * attended_f, axis=-1, keepdims=True)
-    grad_value_part = jnp.einsum(
-        "skqn,skqd->sknd", weights_low, grad_heads, preferred_element_type=jnp.float32
-    )
-    grad_weights = jnp.einsum(
-        "skqd,sknd->skqn", grad_heads, value_all, preferred_element_type=jnp.float32
-    )
-    grad_scores = (weights * (grad_weights - row_delta)).astype(jnp.bfloat16)
-    grad_query = jnp.einsum(
-        "skqn,sknd->skqd", grad_scores, key_all, preferred_element_type=jnp.float32
-    )
-    grad_key_part = (
-        jnp.einsum("skqn,skqd->sknd", grad_scores, queries, preferred_element_type=jnp.float32)
-        * score_scale
-    )
-    grad_kv_part = (
-        jnp.concatenate([grad_key_part, grad_value_part], axis=-1)
-        .astype(jnp.bfloat16)
-        .reshape(seq_count, KV_HEADS, ctx_count, tok_count, 2 * HEAD_DIM)
-        .transpose(1, 2, 0, 3, 4)
-        .reshape(KV_HEADS, *dims, rows_all, 2 * HEAD_DIM)
-    )
+    grad_query, grad_kv_part = pl.pallas_call(
+        attention_grad_kernel,
+        out_shape=[
+            jax.ShapeDtypeStruct(head_shape, jnp.float32),
+            jax.ShapeDtypeStruct(kv_all.shape, jnp.bfloat16),
+        ],
+        compiler_params=local_params,
+        name="attention_grad",
+    )(queries, kv_all, row_pos, key_pos, grad_heads, row_delta, log_total)
+    grad_kv_part = grad_kv_part.reshape(KV_HEADS, *dims, rows_all, 2 * HEAD_DIM)
     grad_kv = (
         scatter_kv(grad_kv_part, dims, 2)
         .transpose(1, 0, 2)

time: 259 us -> 249 us (0.961)
  matrix products: 26.8 us -> 16.2 us
  Pallas kernels: 158 us -> 167 us
  other arithmetic: 17.8 us -> 13.3 us
  local copies, waits for them, and re-layouts: 52.7 us -> 49.2 us
    dot_general x6 -> x0, matrix products: 12.3 us -> none  [the longest x1 3.22 us: local(): jnp.einsum('skqd,sknd->skqn', grad_heads, value_all, preferred_element_ty...]
    concatenate x4 -> x0, local copies, waits for them, and re-layouts: 9.31 us -> none  [local(): jnp.concatenate([grad_key_part, grad_value_part], axis=-1)]
    pallas_call x0 -> x2, Pallas kernels: none -> 8.49 us  [the longest x1 4.62 us: local(): pl.pallas_call(attention_grad_kernel, out_shape=[jax.ShapeDtypeStruct(hea...]
    sub x1 -> x0, other arithmetic: 6.12 us -> none  [local(): weights = jnp.where(visible, jnp.exp(scores - top), 0.0)]
    unnamed x125 -> x107, local copies, waits for them, and re-layouts: 17.1 us -> 23 us
    reshape x2, local copies, waits for them, and re-layouts: 0.36 us -> 2.95 us  [local(): grad_attended.reshape(seq_count, tok_count, HEADS, HEAD_DIM)]
where the time goes in v3:
time: 249 us; the launch traced here: 247 us
  Pallas kernels  167 us (67%)
  local copies, waits for them, and re-layouts  49.2 us (20%)
  matrix products  16.2 us (7%)
  other arithmetic  13.3 us (5%)
    pallas_call x1, Pallas kernels, sum_grads(): pl.pallas_call(functools.partial(sum_grads_kernel, fsdp_count, dims), out...  94.5 us
    unnamed x107, local copies, waits for them, and re-layouts  23 us
    pallas_call x1, Pallas kernels, gather_weights(): pl.pallas_call(functools.partial(weights_kernel, count, fsdp_count, dims)...  22 us
    pallas_call x1, Pallas kernels, gather_kv(): pl.pallas_call(functools.partial(kv_gather_kernel, count, fsdp_count, dim...  21.4 us
    pallas_call x1, Pallas kernels, scatter_kv(): pl.pallas_call(functools.partial(kv_scatter_kernel, dims), out_shape=jax....  18.1 us

profile of v3, /device:TPU:27, one launch (start us, length us, event | category | flops | bytes accessed | tf_op | source)
XLA Modules:
  0.0 247.1 jit_solution(2834033142596136596)
XLA Ops:
  3.8 1.2 reshape.415.refs_3_
  7.5 1.7 copy.226
  9.2 2.2 copy.202.refs_4_
  11.4 22.0 %gather_weights.1 = (bf16[2,288,576]{2,1,0:T(8,128)(2,1)}, bf16[2,288,192]{2,1,0:T(8,128)(2,1)}, bf16[2,288,192]{2,1,0:T(8,128)(2,1)}, bf16[2,1,288]{2,1,0:T(2,128)(2,1)}) custom-call(bf16[288,576]{1,0:T(8,128)(2,1)} %refs_0_.1, bf16[288,192]{1,0:T(8,128)(2,1)} %refs_1_.2, bf16[288,192]{1,0:T(8,128)(2,1)} %refs_2_.2, bf16[1,288]{1,0:T(2,128)(2,1)} %reshape.415.refs_3_), custom_call_target="tpu_custom_call" | custom-call | tf_op jit(solution)/shard_map/gather_weights/pallas_call | solution.py:257
  34.4 1.3 convolution_convert_fusion.1
  40.5 1.2 copy-done.4
  41.7 1.2 copy-done.22
  45.9 21.4 %gather_kv.1 = (bf16[3,4,2,2,128,128]{5,4,3,2,1,0:T(8,128)(2,1)S(1)}, bf16[2,288,576]{2,1,0:T(8,128)(2,1)S(1)}, bf16[2,288,1536]{2,1,0:T(8,128)(2,1)S(1)}, bf16[...) custom-call(bf16[3,128,128]{2,1,0:T(8,128)(2,1)S(1)} %copy-done.30, ...), custom_call_target="tpu_custom_call" | custom-call | tf_op jit(solution)/shard_map/gather_kv/pallas_call | solution.py:293
  69.3 1.3 copy-done.11
  70.7 1.4 copy-done.2
  74.0 3.9 %attention.1 = (f32[2,3,192,64]{3,2,1,0:T(8,128)S(1)}, f32[2,3,192,1]{3,2,1,0:T(8,128)S(1)}) custom-call(bf16[2,3,192,64]{3,2,1,0:T(8,128)(2,1)S(1)} %bitcast.163, bf16[3,16,2,64,128]{4,3,2,1,0:T(8,128)(2,1)S(1)} %bitcast.157, s32[192,1]{1,0:T(8,128)S(1)} %copy-done.24, s32[1,1024]{1,0:T(1,128)S(1)} %fusion.6.key_pos), custom_call_target="tpu_custom_call" | custom-call | tf_op jit(solution)/shard_map/attention/pallas_call | solution.py:665
  79.4 1.9 copy.204
  81.3 1.8 reshape.423
  83.1 2.2 multiply_reduce_fusion.5
  85.4 1.7 fusion.50
  87.1 1.7 copy.225
  88.8 1.5 fusion.21
  90.3 1.6 fusion.20
  92.9 2.4 fusion
  96.0 1.9 multiply_reduce_fusion.1
  101.0 1.8 reshape.429
  102.8 1.2 copy.210
  105.6 4.6 %attention_grad.1 = (f32[2,3,192,64]{3,2,1,0:T(8,128)S(1)}, bf16[3,16,2,64,128]{4,3,2,1,0:T(8,128)(2,1)S(1)}) custom-call(bf16[2,3,192,64]{3,2,1,0:T(8,128)(2,1)S(1)} %bitcast.164, bf16[3,16,2,64,128]{4,3,2,1,0:T(8,128)(2,1)S(1)} %bitcast.158, s32[192,1]{1,0:T(8,128)S(1)} %copy-done.25, s32[1,1024]{1,0:T(1,128)S(1)} %fusion.6.key_pos, ...), custom_call_target="tpu_custom_call" | custom-call | tf_op jit(solution)/shard_map/attention_grad/pallas_call | solution.py:714
  113.6 18.1 %scatter_kv.1 = f32[3,128,128]{2,1,0:T(8,128)S(1)} custom-call(bf16[3,4,2,2,128,128]{5,4,3,2,1,0:T(8,128)(2,1)S(1)} %bitcast.169), custom_call_target="tpu_custom_call" | custom-call | tf_op jit(solution)/shard_map/scatter_kv/pallas_call | solution.py:355
  134.0 1.4 multiply_reduce_fusion.2
  135.7 1.9 add_convert_fusion
  139.0 2.2 pack_grads.1
  141.2 2.9 %copy-done = bf16[2,48,304,128]{3,2,1,0:T(8,128)(2,1)} copy-done((bf16[2,48,304,128]{3,2,1,0:T(8,128)(2,1)}, bf16[2,48,304,128]{3,2,1,0:T(8,128)(2,1)S(1)}, u32[]{:S(2)}) %copy-start) | copy-done | bytes 7471128
  144.1 94.5 %sum_grads.1 = bf16[3,4,2,2,304,128]{5,4,3,2,1,0:T(8,128)(2,1)S(1)} custom-call(bf16[2,3,4,2,2,304,128]{6,5,4,3,2,1,0:T(8,128)(2,1)} %bitcast.149), custom_call_target="tpu_custom_call" | custom-call | tf_op jit(solution)/shard_map/sum_grads/pallas_call | solution.py:429
  240.6 1.6 copy.255
  243.7 1.3 fusion.16
  245.1 2.0 fusion.15
  (179 shorter events, 36.4 us)
Async XLA Ops:
  0.6 33.6 %copy-start.32 = (bf16[2,64,576]{2,1,0:T(8,128)(2,1)S(1)}, bf16[2,64,576]{2,1,0:T(8,128)(2,1)}, u32[]{:S(2)}) copy-start(bf16[2,64,576]{2,1,0:T(8,128)(2,1)} %param.12) | copy-start | bytes 442372
  6.7 32.4 %copy-start.41 = (f32[64,32]{0,1:T(8,128)}, f32[64,32]{0,1:T(8,128)S(1)}, u32[]{:S(2)}) copy-start(f32[64,32]{0,1:T(8,128)S(1)} %get-tuple-element.67) | copy-start | bytes 24580
  6.7 32.4 %copy-start.43 = (f32[64,32]{0,1:T(8,128)}, f32[64,32]{0,1:T(8,128)S(1)}, u32[]{:S(2)}) copy-start(f32[64,32]{0,1:T(8,128)S(1)} %get-tuple-element.68) | copy-start | bytes 24580
  33.4 4.8 %copy-start.34 = (bf16[2,288,576]{2,1,0:T(8,128)(2,1)S(1)}, bf16[2,288,576]{2,1,0:T(8,128)(2,1)}, u32[]{:S(2)}) copy-start(bf16[2,288,576]{2,1,0:T(8,128)(2,1)} %get-tuple-element.26) | copy-start | bytes 1990660
  70.7 1.4 copy-start.2
  77.9 1.6 copy-start.26
  90.3 1.7 copy-start.12
  90.3 1.7 copy-start.38
  92.9 3.1 %copy-start.15 = (bf16[128,1536]{1,0:T(8,128)(2,1)}, bf16[128,1536]{1,0:T(8,128)(2,1)S(1)}, u32[]{:S(2)}) copy-start(bf16[128,1536]{1,0:T(8,128)(2,1)S(1)} %get-tuple-element.52.gate) | copy-start | bytes 1179652
  92.9 3.1 %copy-start.17 = (bf16[128,1536]{1,0:T(8,128)(2,1)}, bf16[128,1536]{1,0:T(8,128)(2,1)S(1)}, u32[]{:S(2)}) copy-start(bf16[128,1536]{1,0:T(8,128)(2,1)S(1)} %get-tuple-element.53.inner) | copy-start | bytes 1179652
  92.9 3.2 %copy-start.13 = (bf16[128,1536]{1,0:T(8,128)(2,1)}, bf16[128,1536]{1,0:T(8,128)(2,1)S(1)}, u32[]{:S(2)}) copy-start(bf16[128,1536]{1,0:T(8,128)(2,1)S(1)} %get-tuple-element.51.up) | copy-start | bytes 1179652
  96.0 2.7 %copy-start.39 = (bf16[2,64,576]{2,1,0:T(8,128)(2,1)S(1)}, bf16[2,64,576]{2,1,0:T(8,128)(2,1)}, u32[]{:S(2)}) copy-start(bf16[2,64,576]{2,1,0:T(8,128)(2,1)} %param.23) | copy-start | bytes 442372
  96.0 3.8 %copy-start.6 = (bf16[2,288,576]{2,1,0:T(8,128)(2,1)S(1)}, bf16[2,288,576]{2,1,0:T(8,128)(2,1)}, u32[]{:S(2)}) copy-start(bf16[2,288,576]{2,1,0:T(8,128)(2,1)} %copy-done.5) | copy-start | bytes 1990660
  97.9 6.0 %copy-start.10 = (f32[2,3,192,64]{3,2,1,0:T(8,128)S(1)}, f32[2,3,192,64]{3,2,1,0:T(8,128)}, u32[]{:S(2)}) copy-start(f32[2,3,192,64]{3,2,1,0:T(8,128)} %copy-done.9) | copy-start | bytes 884740
  98.7 5.6 %copy-start.48 = (f32[128]{0:T(128)}, f32[128]{0:T(128)S(1)}, u32[]{:S(2)}) copy-start(f32[128]{0:T(128)S(1)} %broadcast_multiply_fusion.3) | copy-start | bytes 1540
  99.8 4.7 %copy-start.3 = (bf16[3,4,2,2,128,128]{5,4,3,2,1,0:T(8,128)(2,1)S(1)}, bf16[3,4,2,2,128,128]{5,4,3,2,1,0:T(8,128)(2,1)}, u32[]{:S(2)}) copy-start(bf16[3,4,2,2,128,128]{5,4,3,2,1,0:T(8,128)(2,1)} %copy-done.1) | copy-start | bytes 4718596
  99.8 4.7 %copy-start.8 = (bf16[2,64,3,3,64]{4,1,3,2,0:T(8,128)(2,1)S(1)}, bf16[2,64,3,3,64]{4,1,3,2,0:T(8,128)(2,1)}, u32[]{:S(2)}) copy-start(bf16[2,64,3,3,64]{4,1,3,2,0:T(8,128)(2,1)} %pad_maximum_fusion) | copy-start | bytes 442372
  99.8 4.7 %copy-start.25 = (s32[192,1]{1,0:T(8,128)S(1)}, s32[192,1]{1,0:T(8,128)}, u32[]{:S(2)}) copy-start(s32[192,1]{1,0:T(8,128)} %broadcast_in_dim_tile.4.query_pos) | copy-start | bytes 2308
  111.4 1.3 copy-start.35
  112.1 1.5 copy-start.20
  131.7 2.0 copy-start.40
  133.3 2.3 copy-start.46
  133.3 2.4 copy-start.37
  133.3 2.4 copy-start.49
  133.7 4.0 %copy-start.45 = (bf16[1024]{0:T(1024)(128)(2,1)S(1)}, bf16[1024]{0:T(1024)(128)(2,1)}, u32[]{:S(2)}) copy-start(bf16[1024]{0:T(1024)(128)(2,1)} %pad.11.clone) | copy-start | bytes 6148
  134.0 4.9 %copy-start.14 = (bf16[128,1536]{1,0:T(8,128)(2,1)S(1)}, bf16[128,1536]{1,0:T(8,128)(2,1)}, u32[]{:S(2)}) copy-start(bf16[128,1536]{1,0:T(8,128)(2,1)} %copy-done.13) | copy-start | bytes 1179652
  134.0 4.9 %copy-start.16 = (bf16[128,1536]{1,0:T(8,128)(2,1)S(1)}, bf16[128,1536]{1,0:T(8,128)(2,1)}, u32[]{:S(2)}) copy-start(bf16[128,1536]{1,0:T(8,128)(2,1)} %copy-done.15) | copy-start | bytes 1179652
  134.0 4.9 %copy-start.18 = (bf16[128,1536]{1,0:T(8,128)(2,1)S(1)}, bf16[128,1536]{1,0:T(8,128)(2,1)}, u32[]{:S(2)}) copy-start(bf16[128,1536]{1,0:T(8,128)(2,1)} %copy-done.17) | copy-start | bytes 1179652
  134.0 4.9 %copy-start.21 = (bf16[128,576]{0,1:T(8,128)(2,1)S(1)}, bf16[128,576]{0,1:T(8,128)(2,1)}, u32[]{:S(2)}) copy-start(bf16[128,576]{0,1:T(8,128)(2,1)} %reshape.423) | copy-start | bytes 442372
  134.0 4.9 %copy-start.28 = (bf16[576,128]{1,0:T(8,128)(2,1)S(1)}, bf16[576,128]{1,0:T(8,128)(2,1)}, u32[]{:S(2)}) copy-start(bf16[576,128]{1,0:T(8,128)(2,1)} %copy.226) | copy-start | bytes 442372
  134.0 4.9 %copy-start.29 = (bf16[576,128]{1,0:T(8,128)(2,1)S(1)}, bf16[576,128]{1,0:T(8,128)(2,1)}, u32[]{:S(2)}) copy-start(bf16[576,128]{1,0:T(8,128)(2,1)} %copy.225) | copy-start | bytes 442372
  141.2 2.9 %copy-start = (bf16[2,48,304,128]{3,2,1,0:T(8,128)(2,1)}, bf16[2,48,304,128]{3,2,1,0:T(8,128)(2,1)S(1)}, u32[]{:S(2)}) copy-start(bf16[2,48,304,128]{3,2,1,0:T(8,128)(2,1)S(1)} %pack_grads.1) | copy-start | bytes 22413316
  (18 other events, 18.2 us)
